TPU v7x, 128 devices: a whole 4x4x4 slice. The times are simulated.
128 devices in a mesh: row: 16 (over x, y_lo, core), col: 8 (over y_hi, z).
Axes of the slice: x: 4, y: 4 (y_hi: 2, y_lo: 2; y = y_hi * 2 + y_lo), z: 4, core: 2. Of those that a mesh axis runs over, the one named last changes fastest.
Arguments:
- features: bfloat16 [128, 1024, 3072], P('row', 'col'), may hold values from -6 to 6
- enc_weight: bfloat16 [3072, 64], replicated, may hold values from -0.4375 to 0.4375
- dec_weight: bfloat16 [3072, 64], replicated, may hold values from -0.75 to 0.75
- disc_weight: float32 [64, 64], replicated, may hold values from -0.75 to 0.75
- send_order: int32 [16, 8, 1024], P('row', 'col'), may hold values from 0 to 1023, each once within a row
- recv_order: int32 [16, 8, 1024], P('row', 'col'), may hold values from 0 to 1023, each once within a row
Outputs:
- enc_out: float32 [3072, 64], P(('row', 'col'))
- dec_out: float32 [3072, 64], P(('row', 'col'))
- disc_out: float32 [64, 64], replicated
- embedded_out: float32 [64, 128, 1024], P(None, 'row', 'col')
- logits: float32 [4, 128, 1024], P(None, 'row', 'col')
- proj_grad: bfloat16 [2, 64, 128, 1024], P(None, None, 'row', 'col')
Inputs may be any that keep to these rules, and one draw needn't show every extreme that they name: `send_order`: each device's row of 1024 entries holds every local bin number exactly once. `recv_order`: each device's row of 1024 entries holds every position exactly once.
All inputs are finite; a program needn't handle non-finite values.
Results may differ from a plain program's by a relative error of at most 0.0055.
Values may be sent and summed in bfloat16 or wider, within the bound.
A program may use at most 128 MiB of HBM per device.

v0:
```python
import math

import jax
import jax.numpy as jnp
from jax import lax
from jax.sharding import PartitionSpec as P

RADIUS = 3


RECON_WEIGHT = 10.0
FIRST_WITH_SECOND = (((0,), (1,)), ((), ()))


def padded_2(array, sides, width):
    for axis, dim in sides:
        size, length = (lax.axis_size(axis), array.shape[dim])
        up = [(i, (i + 1) % size) for i in range(size - 1)]
        down = [(j, i) for i, j in up]
        last = lax.slice_in_dim(array, length - width, length, axis=dim)
        leading = lax.slice_in_dim(array, 0, width, axis=dim)
        before = lax.ppermute(last, axis, up)
        after = lax.ppermute(leading, axis, down)
        array = jnp.concatenate([before, array, after], axis=dim)
    return array


def stencil_taps():
    raw_taps = [math.exp(-offset * offset / 12.0) for offset in range(-RADIUS, RADIUS + 1)]
    tap_total = sum(raw_taps)
    return [raw_value / tap_total for raw_value in raw_taps]


def smooth_padded(padded, height_count, width_count):
    tap_list = stencil_taps()
    across = tap_list[0] * padded[..., 0:height_count, :]
    for offset in range(1, 2 * RADIUS + 1):
        across = across + tap_list[offset] * padded[..., offset : offset + height_count, :]
    result = tap_list[0] * across[..., :, 0:width_count]
    for offset in range(1, 2 * RADIUS + 1):
        result = result + tap_list[offset] * across[..., :, offset : offset + width_count]
    return result


def elu_slope(grid_field):
    return jnp.where(
        grid_field > 0, jnp.ones_like(grid_field), jnp.exp(jnp.minimum(grid_field, 0.0))
    )


def per_device(features, enc_weight, dec_weight, disc_weight, send_order, recv_order):
    tile_rows, tile_cols, gene_count = features.shape
    latent_count = enc_weight.shape[1]
    bin_count = tile_rows * tile_cols
    row_devices = lax.axis_size("row")
    col_devices = lax.axis_size("col")
    devices = row_devices * col_devices
    portion = bin_count // devices
    flat_bins = features.reshape(bin_count, gene_count)
    sending = send_order.reshape(bin_count)
    receiving = recv_order.reshape(bin_count)
    projected = lax.dot_general(
        enc_weight, flat_bins, FIRST_WITH_SECOND, preferred_element_type=jnp.float32
    ).astype(jnp.bfloat16)
    outgoing = flat_bins[sending].reshape(devices, portion, gene_count)
    incoming = lax.all_to_all(outgoing, ("row", "col"), split_axis=0, concat_axis=0, tiled=True)
    flat_other = incoming.reshape(bin_count, gene_count)[receiving]
    scrambled = lax.dot_general(
        enc_weight, flat_other, FIRST_WITH_SECOND, preferred_element_type=jnp.float32
    ).astype(jnp.bfloat16)
    stacked = jnp.stack([projected, scrambled]).reshape(2, latent_count, tile_rows, tile_cols)
    padded = padded_2(stacked, (("row", 2), ("col", 3)), RADIUS)
    latent = smooth_padded(padded.astype(jnp.float32), tile_rows, tile_cols)
    embedded = jax.nn.elu(latent)
    padded_embed = padded_2(embedded.astype(jnp.bfloat16), (("row", 2), ("col", 3)), RADIUS).astype(
        embedded.dtype
    )
    spread = smooth_padded(padded_embed, tile_rows, tile_cols)
    summary = jax.nn.sigmoid(spread)
    spread_low = spread[0].reshape(latent_count, bin_count).astype(jnp.bfloat16)
    rebuilt = lax.dot_general(
        spread_low, dec_weight, FIRST_WITH_SECOND, preferred_element_type=jnp.float32
    )
    residual = rebuilt - flat_bins.astype(jnp.float32)
    rec_slope = (2.0 * RECON_WEIGHT / gene_count * residual).astype(jnp.bfloat16)
    rec_back = lax.dot_general(
        dec_weight, rec_slope, FIRST_WITH_SECOND, preferred_element_type=jnp.float32
    )
    dec_grad = lax.psum_scatter(
        lax.dot_general(
            rec_slope, spread_low, FIRST_WITH_SECOND, preferred_element_type=jnp.float32
        ),
        ("row", "col"),
        scatter_dimension=0,
        tiled=True,
    )
    highest = lax.Precision.HIGHEST
    queries = jnp.einsum("kl,blrc->bkrc", disc_weight, summary, precision=highest)
    logit_pos = jnp.sum(embedded[0] * queries[0], axis=0)
    logit_neg = jnp.sum(embedded[1] * queries[0], axis=0)
    logit_cpos = jnp.sum(embedded[1] * queries[1], axis=0)
    logit_cneg = jnp.sum(embedded[0] * queries[1], axis=0)
    logits = jnp.stack([logit_pos, logit_neg, logit_cpos, logit_cneg])
    grad_pos = -jax.nn.sigmoid(-logit_pos)
    grad_neg = jax.nn.sigmoid(logit_neg)
    grad_cpos = -jax.nn.sigmoid(-logit_cpos)
    grad_cneg = jax.nn.sigmoid(logit_cneg)
    embed_grad = jnp.stack(
        [
            grad_pos * queries[0] + grad_cneg * queries[1],
            grad_neg * queries[0] + grad_cpos * queries[1],
        ]
    )
    query_grad = jnp.stack(
        [
            grad_pos * embedded[0] + grad_neg * embedded[1],
            grad_cpos * embedded[1] + grad_cneg * embedded[0],
        ]
    )
    disc_local = jnp.einsum("bkrc,blrc->kl", query_grad, summary, precision=highest)
    disc_grad = lax.psum(disc_local, ("row", "col"))
    summary_grad = jnp.einsum("kl,bkrc->blrc", disc_weight, query_grad, precision=highest)
    spread_grad = summary_grad * summary * (1.0 - summary)
    spread_grad = spread_grad.at[0].add(rec_back.reshape(latent_count, tile_rows, tile_cols))
    padded_spread = padded_2(
        spread_grad.astype(jnp.bfloat16), (("row", 2), ("col", 3)), RADIUS
    ).astype(spread_grad.dtype)
    embed_total = embed_grad + smooth_padded(padded_spread, tile_rows, tile_cols)
    latent_grad = embed_total * elu_slope(latent)
    padded_latent = padded_2(
        latent_grad.astype(jnp.bfloat16), (("row", 2), ("col", 3)), RADIUS
    ).astype(latent_grad.dtype)
    proj_grad = smooth_padded(padded_latent, tile_rows, tile_cols).astype(jnp.bfloat16)
    own_grad = proj_grad[0].reshape(latent_count, bin_count)
    shuffled_grad = proj_grad[1].reshape(latent_count, bin_count)
    first_term = lax.dot_general(
        flat_bins, own_grad, FIRST_WITH_SECOND, preferred_element_type=jnp.float32
    )
    second_term = lax.dot_general(
        flat_other, shuffled_grad, FIRST_WITH_SECOND, preferred_element_type=jnp.float32
    )
    enc_grad = lax.psum_scatter(
        first_term + second_term, ("row", "col"), scatter_dimension=0, tiled=True
    )
    enc_square = jnp.sum(enc_grad * enc_grad)
    dec_square = jnp.sum(dec_grad * dec_grad)
    enc_total, dec_total = lax.psum((enc_square, dec_square), ("row", "col"))
    weight_entries = gene_count * latent_count
    enc_out = enc_grad * lax.rsqrt(enc_total / weight_entries + 1e-06)
    dec_out = dec_grad * lax.rsqrt(dec_total / weight_entries + 1e-06)
    disc_out = disc_grad * lax.rsqrt(jnp.mean(disc_grad * disc_grad) + 1e-06)
    return (enc_out, dec_out, disc_out, embedded[0], logits, proj_grad)


def solution(mesh):
    in_specs = (P("row", "col", None), P(), P(), P(), P("row", "col", None), P("row", "col", None))
    out_specs = (
        P(("row", "col"), None),
        P(("row", "col"), None),
        P(),
        P(None, "row", "col"),
        P(None, "row", "col"),
        P(None, None, "row", "col"),
    )
    return jax.shard_map(
        per_device, mesh=mesh, in_specs=in_specs, out_specs=out_specs, check_vma=False
    )
```

profile of v0, /device:TPU:1, one launch (start us, length us, event | category | flops | bytes accessed | tf_op | source)
XLA Modules:
  0.0 1132.8 jit_solution(804670156894733611)
XLA Ops:
  7.2 0.7 compare_select_fusion.4
  7.9 15.8 %gather_fusion = bf16[1024,3072]{1,0:T(8,128)(2,1)} fusion(bf16[1024,3072]{1,0:T(8,128)(2,1)} %bitcast.103, s32[1024]{0:T(1024)S(1)} %broadcast_clamp_fusion.1), kind=kCustom, calls=%fused_computation | custom fusion | bytes 12587008 | tf_op jit(solution)/shard_map/gather | solution.py:65
  23.7 11.9 %all-to-all-start = ((bf16[128,8,3072]{2,1,0:T(8,128)(2,1)}), bf16[128,8,3072]{2,1,0:T(8,128)(2,1)}, u32[]{:S(2)}, u32[]{:S(2)}) async-start(bf16[128,8,3072]{2,1,0:T(8,128)(2,1)} %bitcast.111), calls=%async_computation | async-start | bytes 12582912 | tf_op jit(solution)/shard_map/all_to_all | solution.py:66
  35.7 4.8 fusion.3
  40.6 71.6 %all-to-all-done = bf16[128,8,3072]{2,1,0:T(8,128)(2,1)} async-done(((bf16[128,8,3072]{2,1,0:T(8,128)(2,1)}), bf16[128,8,3072]{2,1,0:T(8,128)(2,1)}, u32[]{:S(2)}, u32[]{:S(2)}) %all-to-all-start) | async-done | bytes 6291488 | tf_op jit(solution)/shard_map/all_to_all | solution.py:66
  112.2 15.8 %gather_fusion.1 = bf16[1024,3072]{1,0:T(8,128)(2,1)} fusion(bf16[1024,3072]{1,0:T(8,128)(2,1)} %bitcast.4, s32[1024]{0:T(1024)S(1)} %broadcast_clamp_fusion), kind=kCustom, calls=%fused_computation.1 | custom fusion | bytes 12587008 | tf_op jit(solution)/shard_map/gather | solution.py:67
  128.0 4.8 fusion.4
  132.9 2.3 collective-permute-start
  135.2 3.1 collective-permute-start.1
  138.3 2.8 collective-permute-done.1
  141.4 3.6 collective-permute-start.2
  145.0 1.3 collective-permute-start.3
  146.3 6.7 collective-permute-done.2
  153.0 4.1 collective-permute-done.3
  158.1 0.9 fusion.77
  159.0 2.2 collective-permute-start.4
  161.2 2.2 collective-permute-start.5
  163.4 5.1 collective-permute-done.5
  168.7 3.4 collective-permute-start.6
  172.2 1.5 collective-permute-start.7
  173.9 5.0 collective-permute-done.6
  178.9 4.4 collective-permute-done.7
  183.2 0.5 maximum_convert_fusion.1
  184.2 0.9 fusion.46
  185.4 0.7 convolution_bitcast_fusion.2
  186.3 1.8 multiply_convert_fusion
  188.1 2.0 convolution_bitcast_fusion.3
  190.1 0.6 copy-done.1
  191.1 0.7 fusion.2
  192.0 6.0 collective-permute-start.8
  198.0 1.9 collective-permute-start.9
  200.0 5.0 collective-permute-done.9
  205.3 4.5 collective-permute-start.10
  209.8 1.3 collective-permute-start.11
  211.1 5.3 collective-permute-done.10
  216.4 4.4 collective-permute-done.11
  220.8 0.5 maximum_convert_fusion.2
  221.8 0.9 fusion.31
  222.7 4.7 collective-permute-start.12
  227.4 1.9 collective-permute-start.13
  229.3 5.0 collective-permute-done.13
  234.6 5.3 collective-permute-start.14
  239.9 1.5 collective-permute-start.15
  241.4 5.1 collective-permute-done.14
  246.5 4.4 collective-permute-done.15
  251.8 0.9 fusion.33
  253.1 0.8 slice-done.3
  253.9 1.2 fusion.63
  255.1 2.2 fusion
  257.3 5.8 fusion.68
  263.1 0.9 copy.39
  264.0 0.6 pad_maximum_fusion.7
  264.6 0.7 convolution_bitcast_fusion.4
  265.3 149.2 %all-reduce.5.cloned.1.call-done = f32[3072,64]{0,1:T(8,128)} async-done(((f32[3072,64]{0,1:T(8,128)}), f32[3072,64]{0,1:T(8,128)}) %all-reduce.5.cloned.1.call-update) | async-done | bytes 786448
  414.5 1.5 multiply_reduce_fusion.1
  416.0 624.4 %reduce-scatter.6.cloned.1.call-done = f32[24,64]{1,0:T(8,128)} async-done(((f32[3072,64]{1,0:T(8,128)}), f32[24,64]{1,0:T(8,128)}) %reduce-scatter.6.cloned.1.call-update) | async-done | bytes 6160
  1040.5 1.3 multiply_reduce_fusion.2
  1041.8 0.9 copy.40
  1042.7 77.1 %all-reduce.2 = (f32[]{:T(128)}, f32[]{:T(128)}, f32[64,64]{1,0:T(8,128)S(1)}) all-reduce(f32[]{:T(128)} %multiply_reduce_fusion.1, f32[]{:T(128)} %multiply_reduce_fusion.2, f32[64,64]{1,0:T(8,128)S(1)} %convolution_bitcast_fusion.4), channel_id=1, replica_groups=mesh['row'=16,'col'=8] {'row','col'}, use_global_device_ids=true, to_apply=%region_6.7 | all-reduce | flops 4098 | bytes 32784 | tf_op jit(solution)/shard_map/psum | solution.py:147
  1121.1 0.9 dynamic-slice_multiply_fusion
  1122.1 0.7 copy.38
  1122.7 0.6 multiply_reduce_fusion
  1124.0 0.6 broadcast_multiply_fusion
  1124.7 1.3 broadcast_multiply_fusion.1
  (64 shorter events, 5.5 us)
Async XLA Ops:
  7.2 179.0 %copy-start = (bf16[3072,64]{0,1:T(8,128)(2,1)S(1)}, bf16[3072,64]{0,1:T(8,128)(2,1)}, u32[]{:S(2)}) copy-start(bf16[3072,64]{0,1:T(8,128)(2,1)} %param.10) | copy-start | bytes 1179652
  23.7 12.0 %copy-start.2 = (bf16[3072,64]{0,1:T(8,128)(2,1)S(1)}, bf16[3072,64]{0,1:T(8,128)(2,1)}, u32[]{:S(2)}) copy-start(bf16[3072,64]{0,1:T(8,128)(2,1)} %param.9) | copy-start | bytes 1179652
  23.7 88.5 %all-to-all-start = ((bf16[128,8,3072]{2,1,0:T(8,128)(2,1)}), bf16[128,8,3072]{2,1,0:T(8,128)(2,1)}, u32[]{:S(2)}, u32[]{:S(2)}) async-start(bf16[128,8,3072]{2,1,0:T(8,128)(2,1)} %bitcast.111), calls=%async_computation | async-start | bytes 12582912 | tf_op jit(solution)/shard_map/all_to_all | solution.py:66
  35.6 4.9 copy-start.3
  35.6 378.9 %all-reduce.5.cloned.1.call-start = ((), (), s32[]{:S(2)}) async-start(), calls=%async_computation.2 | async-start | bytes 1572864
  132.9 5.4 collective-permute-start
  135.2 5.9 collective-permute-start.1
  141.4 11.6 %collective-permute-start.2 = (bf16[2,64,14,3]{3,1,2,0:T(8,128)(2,1)S(1)}, bf16[2,64,14,3]{3,1,2,0:T(8,128)(2,1)S(1)}, u32[]{:S(2)}, u32[]{:S(2)}) collective-permute-start(bf16[2,64,14,3]{3,1,2,0:T(8,128)(2,1)S(1)} %get-tuple-element.56), channel_id=1, source_target_pairs={{0,1},{1,2},{2,3},{3,4},{4,5},{5,6},{6,7},{8,9},{9,10},{10,11},{11... | collective-permute-start | bytes 32264 | tf_op jit(solution)/shard_map/ppermute | solution.py:22
  145.0 12.2 %collective-permute-start.3 = (bf16[2,64,14,3]{3,1,2,0:T(8,128)(2,1)S(1)}, bf16[2,64,14,3]{3,1,2,0:T(8,128)(2,1)S(1)}, u32[]{:S(2)}, u32[]{:S(2)}) collective-permute-start(bf16[2,64,14,3]{3,1,2,0:T(8,128)(2,1)S(1)} %get-tuple-element.57), channel_id=1, source_target_pairs={{1,0},{2,1},{3,2},{4,3},{5,4},{6,5},{7,6},{9,8},{10,9},{11,10},{12... | collective-permute-start | bytes 32264 | tf_op jit(solution)/shard_map/ppermute | solution.py:23
  159.0 4.3 collective-permute-start.4
  161.2 7.3 collective-permute-start.5
  168.7 10.1 collective-permute-start.6
  172.2 11.0 collective-permute-start.7
  183.2 2.9 slice-start
  183.8 2.5 slice-start.1
  184.2 1.2 copy-start.4
  188.1 2.7 copy-start.1
  192.0 8.0 collective-permute-start.8
  198.0 7.0 collective-permute-start.9
  205.3 11.1 collective-permute-start.10
  209.8 11.0 collective-permute-start.11
  222.7 6.6 collective-permute-start.12
  227.4 7.0 collective-permute-start.13
  234.6 11.9 %collective-permute-start.14 = (bf16[2,64,14,3]{3,1,2,0:T(8,128)(2,1)S(1)}, bf16[2,64,14,3]{3,1,2,0:T(8,128)(2,1)S(1)}, u32[]{:S(2)}, u32[]{:S(2)}) collective-permute-start(bf16[2,64,14,3]{3,1,2,0:T(8,128)(2,1)S(1)} %get-tuple-element.50), channel_id=1, source_target_pairs={{0,1},{1,2},{2,3},{3,4},{4,5},{5,6},{6,7},{8,9},{9,10},{10,11},{11... | collective-permute-start | bytes 32264 | tf_op jit(solution)/shard_map/ppermute | solution.py:22
  239.9 11.0 collective-permute-start.15
  250.9 2.2 slice-start.2
  251.4 2.5 slice-start.3
  257.3 783.2 %reduce-scatter.6.cloned.1.call-start = ((), (), s32[]{:S(2)}) async-start(), calls=%async_computation.3 | async-start | bytes 1585152
Sparse Core Ops, SparseCore 0:
  257.4 157.0 all-reduce.4
  416.9 623.5 reduce-scatter.5
where the time goes:
time: 1130 us
  waiting for transfers between devices  903 us (80%)
  blocking collectives  77.1 us (7%)
  starting transfers between devices  58.7 us (5%)
  local copies, waits for them, and re-layouts  37.3 us (3%)
  matrix products  24.7 us (2%)
  between operations  16.7 us (1%)
  other arithmetic  15.8 us (1%)
    unnamed x4, waiting for transfers between devices  774 us
    psum x1, blocking collectives, per_device(): enc_total, dec_total = lax.psum((enc_square, dec_square), ('row', 'col'))  77.1 us
    all_to_all x1, waiting for transfers between devices, per_device(): lax.all_to_all(outgoing, ('row', 'col'), split_axis=0, concat_axis=0, til...  71.6 us
    ppermute x8, waiting for transfers between devices, padded_2(): after = lax.ppermute(leading, axis, down)  35.2 us
    ppermute x8, starting transfers between devices, padded_2(): before = lax.ppermute(last, axis, up)  32 us
  transfers between devices with their start and end apart: 19, of which 15 were waited for; matrix products, arithmetic and copies ran while one was open for 1% of the time, Pallas kernels for 0%

commit v1 on v0

v1 whole, which is shorter than its diff:
```python
import functools
import math

import jax
import jax.numpy as jnp
from jax import lax
from jax.experimental import pallas as pl
from jax.experimental.pallas import tpu as pltpu
from jax.sharding import PartitionSpec as P

RADIUS = 3
RECON_WEIGHT = 10.0
LANES = 128
EDGE = 16
SIDE = 8
MESH = pl.DeviceIdType.MESH
F32 = jnp.float32
BF16 = jnp.bfloat16
DIRECTIONS = ((-1, 0), (1, 0), (0, -1), (0, 1), (-1, -1), (-1, 1), (1, -1), (1, 1))
OPPOSITE = (1, 0, 3, 2, 7, 6, 5, 4)
ROUNDS = 5
PACKED = {0: 0, 2: 1}
CHUNKS = 4


def stencil_taps():
    raw_taps = [math.exp(-offset * offset / 12.0) for offset in range(-RADIUS, RADIUS + 1)]
    tap_total = sum(raw_taps)
    return [raw_value / tap_total for raw_value in raw_taps]


def dot(a, b, ca=1, cb=0):
    return lax.dot_general(a, b, (((ca,), (cb,)), ((), ())), preferred_element_type=F32)


def split_2(value):
    high = value.astype(BF16)
    low = (value - high.astype(F32)).astype(BF16)
    return jnp.concatenate([high, low], axis=1)


def kernel(
    n_row,
    n_col,
    feat_hbm,
    enc_hbm,
    dec_hbm,
    disc_hbm,
    send_hbm,
    recv_hbm,
    enc_hbm_out,
    dec_hbm_out,
    disc_hbm_out,
    emb_hbm_out,
    log_hbm_out,
    pg_hbm_out,
    enc_out,
    dec_out,
    disc_out,
    emb_out,
    log_out,
    pg_out,
    x,
    discw,
    orders,
    wcat,
    wtwice,
    gram2,
    bd_nt,
    bd_nn,
    send_pick,
    recv_pick,
    recv_pick_t,
    xp,
    xp_low,
    ex_src,
    ex_dst,
    pads,
    tmp,
    hsrc,
    h_row,
    h_col,
    h_corner,
    pack_src,
    h_pack,
    lat,
    emb,
    spread,
    summ,
    s_low,
    back,
    grads_2,
    summ_2,
    mix,
    eg,
    pg_low,
    lt,
    own,
    rs1_src,
    rs1_dst,
    rs2_src,
    rs2_dst,
    disc_src,
    disc_a,
    disc_bsrc,
    disc_b,
    disc_full,
    norm_src,
    norm_a,
    norm_bsrc,
    norm_b,
    stage,
    dec_sum,
    load_sem,
    feat_sem,
    hs_sem,
    hr_sem,
    as_sem,
    ar_sem,
    r1s_sem,
    r1r_sem,
    r2s_sem,
    r2r_sem,
    ds_sem,
    dr_sem,
    ns_sem,
    nr_sem,
    meet_sem,
    out_sem,
):
    n_dev = n_row * n_col
    bins, genes = x.shape
    rows = bins // LANES
    lats = discw.shape[1]
    portion = bins // n_dev
    n_group = n_row // 2
    n_pair = n_group // 2
    per_dev = genes // n_dev
    span = genes // n_group
    per_group = 2 * n_col
    part = lats // n_col
    slope_scale = 2.0 * RECON_WEIGHT / genes
    tap = stencil_taps()
    chunk = bins // CHUNKS

    r = lax.axis_index("row")
    c = lax.axis_index("col")
    me = r * n_col + c
    my_group = r // 2
    lane = lax.broadcasted_iota(jnp.int32, (1, LANES), 1)
    first = lane < lats

    outs = [
        pltpu.make_async_copy(a, b, out_sem.at[i])
        for i, (a, b) in enumerate(
            [
                (enc_out, enc_hbm_out),
                (dec_out, dec_hbm_out),
                (disc_out, disc_hbm_out),
                (emb_out, emb_hbm_out),
                (log_out, log_hbm_out),
                (pg_out, pg_hbm_out),
            ]
        )
    ]

    def swap(value):
        return pltpu.roll(value, lats, value.ndim - 1)

    def halo_buffer(turn, way):
        if way < 2:
            return h_row.at[turn, way]
        if way < 4:
            return h_col.at[turn, way - 2]
        return h_corner.at[turn, way - 4]

    def halo_copy(turn, way):
        dr, dc = DIRECTIONS[way]
        row_part = pl.ds(0, RADIUS) if dr < 0 else pl.ds(rows - RADIUS, RADIUS) if dr else pl.ds(0, rows)
        col_part = pl.ds(0, EDGE) if dc < 0 else pl.ds(LANES - EDGE, EDGE) if dc else pl.ds(0, LANES)
        if way < 2 and turn in PACKED:
            source = pack_src.at[PACKED[turn], way]
            target = h_pack.at[PACKED[turn], OPPOSITE[way]]
        else:
            source = hsrc.at[turn, row_part, col_part]
            target = halo_buffer(turn, OPPOSITE[way])
        return pltpu.make_async_remote_copy(
            src_ref=source,
            dst_ref=target,
            send_sem=hs_sem.at[turn, way],
            recv_sem=hr_sem.at[turn, OPPOSITE[way]],
            device_id=(r + dr, c + dc),
            device_id_type=MESH,
        )

    def present(way):
        dr, dc = DIRECTIONS[way]
        tests = []
        if dr < 0:
            tests.append(r > 0)
        if dr > 0:
            tests.append(r < n_row - 1)
        if dc < 0:
            tests.append(c > 0)
        if dc > 0:
            tests.append(c < n_col - 1)
        return functools.reduce(jnp.logical_and, tests)

    def halo_start(turn):
        for way in range(8):

            @pl.when(present(way))
            def _():
                halo_copy(turn, way).start()

    def halo_take(turn):
        pad = pads.at[turn % 2]
        for way in range(8):

            @pl.when(present(way))
            def _():
                halo_copy(turn, OPPOSITE[way]).wait_recv()

        left, right = slice(0, SIDE), slice(SIDE + LANES, LANES + 2 * SIDE)
        top, bottom = slice(0, RADIUS), slice(RADIUS + rows, rows + 2 * RADIUS)
        for way, part in ((0, top), (1, bottom)):
            if turn in PACKED:
                packed = h_pack[PACKED[turn], way].astype(F32)
                halves = (packed, swap(packed)) if turn == 0 else (swap(packed), packed)
                pad[part, SIDE : SIDE + LANES // 2, :] = halves[0]
                pad[part, SIDE + LANES // 2 : SIDE + LANES, :] = halves[1]
            else:
                pad[part, SIDE : SIDE + LANES, :] = h_row[turn, way].astype(F32)
            pad[part, left, :] = h_corner[turn, 2 * way].astype(F32)[:, EDGE - SIDE :, :]
            pad[part, right, :] = h_corner[turn, 2 * way + 1].astype(F32)[:, :SIDE, :]
        own_rows = slice(RADIUS, RADIUS + rows)
        pad[own_rows, left, :] = h_col[turn, 0].astype(F32)[:, EDGE - SIDE :, :]
        pad[own_rows, right, :] = h_col[turn, 1].astype(F32)[:, :SIDE, :]

    def halo_finish(turn):
        for way in range(8):

            @pl.when(present(way))
            def _():
                halo_copy(turn, way).wait_send()

    def stencil(turn, then):
        pad = pads.at[turn % 2]
        for t in range(0, LANES + 2 * SIDE, SIDE):
            block = pad[:, t : t + SIDE, :]
            across = tap[RADIUS] * block[RADIUS : RADIUS + rows]
            for k in range(1, RADIUS + 1):
                across += tap[RADIUS + k] * (
                    block[RADIUS - k : RADIUS - k + rows] + block[RADIUS + k : RADIUS + k + rows]
                )
            tmp[:, t : t + SIDE, :] = across
        for i in range(rows):
            total = tap[RADIUS] * tmp[i, SIDE : SIDE + LANES, :]
            for k in range(1, RADIUS + 1):
                total += tap[RADIUS + k] * (
                    tmp[i, SIDE - k : SIDE - k + LANES, :] + tmp[i, SIDE + k : SIDE + k + LANES, :]
                )
            then(i, total)

    def put(turn, i, value):
        pads[turn % 2, i + RADIUS, SIDE : SIDE + LANES, :] = value
        low = value.astype(BF16)
        if turn not in PACKED:
            hsrc[turn, i] = low
            return
        hsrc[turn, i, 0:EDGE, :] = low[0:EDGE, :]
        hsrc[turn, i, LANES - EDGE :, :] = low[LANES - EDGE :, :]
        front, rear = value[: LANES // 2, :], value[LANES // 2 :, :]
        if turn == 0:
            packed = jnp.where(first, front, swap(rear)).astype(BF16)
        else:
            packed = jnp.where(first, swap(front), rear).astype(BF16)
        if i < RADIUS:
            pack_src[PACKED[turn], 0, i] = packed
        if i >= rows - RADIUS:
            pack_src[PACKED[turn], 1, i - (rows - RADIUS)] = packed

    loads = [
        pltpu.make_async_copy(a, b, load_sem.at[i])
        for i, (a, b) in enumerate(
            [
                (send_hbm, orders.at[0]),
                (recv_hbm, orders.at[1]),
                (dec_hbm, wcat.at[pl.ds(0, lats)]),
                (enc_hbm, wcat.at[pl.ds(lats, lats)]),
                (dec_hbm, wtwice.at[pl.ds(0, lats)]),
                (dec_hbm, wtwice.at[pl.ds(lats, lats)]),
                (disc_hbm, discw),
            ]
        )
    ]
    for load in loads[:4]:
        load.start()
    feats = []
    for i in range(rows):
        piece = pl.ds(i * LANES, LANES)
        copy = pltpu.make_async_copy(feat_hbm.at[piece], x.at[piece], feat_sem.at[i])
        copy.start()
        feats.append(copy)
    for load in loads[4:]:
        load.start()

    barrier = pltpu.get_barrier_semaphore()

    def greet_row(k, carry):
        other = lax.rem(r + k, n_row)
        pl.semaphore_signal(barrier, inc=1, device_id=(other, c), device_id_type=MESH)
        return carry

    def greet_col(k, carry):
        other = lax.rem(c + k, n_col)
        pl.semaphore_signal(barrier, inc=1, device_id=(r, other), device_id_type=MESH)
        return carry

    lax.fori_loop(1, n_row, greet_row, 0)
    lax.fori_loop(1, n_col, greet_col, 0)

    def build_send():
        for a in range(rows):
            line = orders[0, a : a + 1, :].astype(F32)
            column = jnp.broadcast_to(line, (LANES, LANES)).T
            for t in range(rows):
                index = (lane + t * LANES).astype(F32)
                send_pick[a * LANES : (a + 1) * LANES, t * LANES : (t + 1) * LANES] = jnp.where(
                    column == index, 1.0, 0.0
                ).astype(BF16)

    def build_recv():
        def body(a, carry):
            line = orders[1, pl.ds(a, 1), :].astype(F32)
            column = jnp.broadcast_to(line, (LANES, LANES)).T
            for t in range(rows):
                index = (lane + t * LANES).astype(F32)
                recv_pick[
                    pl.ds(pl.multiple_of(a * LANES, LANES), LANES), t * LANES : (t + 1) * LANES
                ] = jnp.where(column == index, 1.0, 0.0).astype(BF16)
            return carry

        lax.fori_loop(0, rows, body, 0)

    def build_recv_t():
        def body(t, carry):
            index = (lax.broadcasted_iota(jnp.int32, (LANES, 1), 0) + t * LANES).astype(F32)
            for a in range(rows):
                line = orders[1, a : a + 1, :].astype(F32)
                recv_pick_t[
                    pl.ds(pl.multiple_of(t * LANES, LANES), LANES), a * LANES : (a + 1) * LANES
                ] = jnp.where(line == index, 1.0, 0.0).astype(BF16)
            return carry

        lax.fori_loop(0, rows, body, 0)

    def ex_copy(which, k):
        other = lax.rem(me + k, n_dev)
        return pltpu.make_async_remote_copy(
            src_ref=ex_src.at[which, other],
            dst_ref=ex_dst.at[which, me],
            send_sem=as_sem.at[which],
            recv_sem=ar_sem.at[which],
            device_id=(other // n_col, lax.rem(other, n_col)),
            device_id_type=MESH,
        )

    def peers(count, make):
        def body(k, carry):
            make(k).start()
            return carry

        lax.fori_loop(1, count, body, 0)

    def drain(ref, count, send_sem, recv_sem):
        most = ref.at[pl.ds(0, count - 1)]
        pltpu.make_async_copy(most, most, recv_sem).wait()
        pltpu.make_async_copy(most, most, send_sem).wait()

    def ex_start(which):
        peers(n_dev, functools.partial(ex_copy, which))
        ex_dst[which, me] = ex_src[which, me]

    def ex_wait(which):
        drain(ex_dst.at[which], n_dev, as_sem.at[which], ar_sem.at[which])
        return ex_dst[which].reshape(bins, LANES)

    rs2_src[...] = jnp.zeros_like(rs2_src)
    loads[0].wait()
    loads[1].wait()
    build_send()
    for way in range(8):

        @pl.when(jnp.logical_not(present(way)))
        def _():
            for turn in range(ROUNDS):
                if way < 2 and turn in PACKED:
                    empty = h_pack.at[PACKED[turn], way]
                else:
                    empty = halo_buffer(turn, way)
                empty[...] = jnp.zeros_like(empty)

    loads[2].wait()
    loads[3].wait()

    for i in range(2):
        for k in range(rows // 2):
            feats[i * (rows // 2) + k].wait()
        piece = slice(i * (bins // 2), (i + 1) * (bins // 2))
        acc = dot(x[piece, :], wcat[...], 1, 1)
        xp[piece, :] = acc
        xp_low[piece, :] = acc.astype(BF16)
    outgoing = dot(send_pick[...], xp_low[...])
    ex_src[0] = outgoing.astype(BF16).reshape(n_dev, portion, LANES)

    pl.semaphore_wait(barrier, n_row + n_col - 2)

    def greet_meet(k, carry):
        other = lax.rem(c + k, n_col)
        pl.semaphore_signal(meet_sem, inc=1, device_id=(r, other), device_id_type=MESH)
        return carry

    lax.fori_loop(1, n_col, greet_meet, 0)
    pl.semaphore_wait(meet_sem, n_col - 1)

    ex_start(0)

    for i in range(rows):
        piece = slice(i * LANES, (i + 1) * LANES)
        put(0, i, swap(xp_low[piece, :].astype(F32)))
    halo_start(0)
    build_recv()
    def elu(value):
        return jnp.where(value > 0, value, jnp.exp(jnp.minimum(value, 0.0)) - 1.0)

    def first_latent(i, value):
        lat[i] = value
        emb[i] = elu(value)

    halo_take(0)
    stencil(0, first_latent)

    scrambled = dot(recv_pick[...], ex_wait(0))
    for i in range(rows):
        put(1, i, jnp.where(first, emb[i], scrambled[i * LANES : (i + 1) * LANES, :]))
    halo_start(1)
    build_recv_t()
    gram = dot(wcat[0:lats, :], wcat[0:lats, :], 1, 1)
    gram_high = gram.astype(BF16)
    gram_low = (gram - gram_high.astype(F32)).astype(BF16)
    gram2[...] = jnp.zeros_like(gram2)
    gram2[0:lats, 0:lats] = gram_high
    gram2[lats:, 0:lats] = gram_low

    def first_spread(i, value):
        out = elu(value)
        lat[i] = jnp.where(first, lat[i], value)
        emb[i] = jnp.where(first, emb[i], out)
        put(2, i, out)
        spread[i] = value

    halo_take(1)
    stencil(1, first_spread)
    halo_start(2)
    for i in range(rows):
        value = spread[i]
        here = slice(i * LANES, (i + 1) * LANES)
        low = value.astype(BF16).astype(F32)
        summ[i] = jax.nn.sigmoid(value)
        s_low[here, :] = jnp.where(first, low, swap(low)).astype(BF16)
        lt[0:lats, here] = low.T[0:lats, :].astype(BF16)

    back[...] = slope_scale * (
        dot(s_low[...], gram2[...]) - jnp.where(first, xp[...], 0.0)
    )

    def rs1_copy(which, group):
        return pltpu.make_async_remote_copy(
            src_ref=rs1_src.at[which, group],
            dst_ref=rs1_dst.at[which, my_group],
            send_sem=r1s_sem.at[which],
            recv_sem=r1r_sem.at[which],
            device_id=(2 * group + lax.rem(r, 2), c),
            device_id_type=MESH,
        )

    def rs1_run(which, product):
        for k in range(n_pair):
            pair = lax.rem(my_group // 2 + 1 + k, n_pair)
            where = pl.ds(pl.multiple_of(pair * (2 * span), LANES), 2 * span)
            value = product(where).astype(BF16)
            for j in range(2):
                rs1_src[which, 2 * pair + j] = value[:, j * span : (j + 1) * span]
            if k < n_pair - 1:
                for j in range(2):
                    rs1_copy(which, 2 * pair + j).start()
            else:
                rs1_copy(which, my_group + 1 - 2 * lax.rem(my_group, 2)).start()

    def rs1_finish(which):
        seven = rs1_dst.at[which, pl.ds(0, n_group - 1)]
        pltpu.make_async_copy(seven, seven, r1r_sem.at[which]).wait()
        pltpu.make_async_copy(seven, seven, r1s_sem.at[which]).wait()
        rs1_dst[which, my_group] = rs1_src[which, my_group]
        total = rs1_dst[which, 0].astype(F32)
        for group in range(1, n_group):
            total += rs1_dst[which, group].astype(F32)
        for k in range(span // LANES):
            rs2_src[which, k * LANES : (k + 1) * LANES, 0:lats] = total[
                :, k * LANES : (k + 1) * LANES
            ].T

    mine = lax.rem(r, 2) * n_col + c

    def gene_part(index):
        return pl.ds(pl.multiple_of(index * per_dev, 8), per_dev)

    def rs2_start(which):
        def body(k, carry):
            other = lax.rem(mine + k, per_group)
            pltpu.make_async_remote_copy(
                src_ref=rs2_src.at[which, gene_part(other)],
                dst_ref=rs2_dst.at[which, mine],
                send_sem=r2s_sem.at[which],
                recv_sem=r2r_sem.at[which],
                device_id=((r // 2) * 2 + other // n_col, lax.rem(other, n_col)),
                device_id_type=MESH,
            ).start()
            return carry

        rs2_dst[which, mine] = rs2_src[which, gene_part(mine), :]
        lax.fori_loop(1, per_group, body, 0)

    def rs2_finish(which):
        most = rs2_dst.at[which, pl.ds(0, per_group - 1)]
        pltpu.make_async_copy(most, most, r2r_sem.at[which]).wait()
        pltpu.make_async_copy(most, most, r2s_sem.at[which]).wait()
        total = rs2_dst[which, 0]
        for k in range(1, per_group):
            total += rs2_dst[which, k]
        return jnp.where(first, total, 0.0)

    loads[4].wait()
    loads[5].wait()
    square = dot(lt[0:lats, :], s_low[...])
    square_high = square.astype(BF16).astype(F32)
    square2 = jnp.where(first, square_high, square - square_high).astype(BF16)
    rs1_run(
        0,
        lambda where: slope_scale
        * (dot(square2, wtwice[:, where]) - dot(lt[0:lats, :], x[:, where])),
    )

    loads[6].wait()
    wide = jnp.concatenate([discw[...], jnp.zeros_like(discw)], axis=1)
    block = jnp.concatenate([wide, pltpu.roll(wide, lats, 1)], axis=0)
    block_high = block.astype(BF16)
    block_low = (block - block_high.astype(F32)).astype(BF16)
    for u in range(2):
        one = slice(u * LANES, (u + 1) * LANES)
        bd_nt[0:LANES, one] = block_high
        bd_nt[LANES:, one] = block_low
        bd_nn[one, 0:LANES] = block_high
        bd_nn[one, LANES:] = block_low
    for i in range(rows):
        stage[:, i, :] = emb[i].T
    emb_out[...] = stage[0:lats]
    outs[3].start()
    halo_take(2)

    def to_summary(i, value):
        summ[i] = jnp.where(first, summ[i], jax.nn.sigmoid(value))

    stencil(2, to_summary)

    half_sum = jnp.where(
        (lax.broadcasted_iota(jnp.int32, (LANES, LANES), 0) < lats)
        == (lax.broadcasted_iota(jnp.int32, (LANES, LANES), 1) < lats),
        1.0,
        0.0,
    ).astype(BF16)
    half_sum2 = jnp.concatenate([half_sum, half_sum], axis=0)

    step = rows // CHUNKS
    for i in range(CHUNKS):
        piece = slice(i * step, (i + 1) * step)
        summary = summ[piece].reshape(chunk, LANES)
        embedded = emb[piece].reshape(chunk, LANES)
        swapped = swap(embedded)
        summary_2 = split_2(summary)
        wide_q = dot(summary_2, bd_nt[...], 1, 1)
        queries = wide_q[:, :LANES] + wide_q[:, LANES:]
        logit_same = dot(split_2(embedded * queries), half_sum2)
        logit_other = dot(split_2(swapped * queries), half_sum2)
        grad_same = -jax.nn.sigmoid(-logit_same)
        grad_other = jax.nn.sigmoid(logit_other)
        embed_grad = grad_same * queries + swap(grad_other * queries)
        query_grad = grad_same * embedded + grad_other * swapped
        query_grad_2 = split_2(query_grad)
        here = slice(i * chunk, (i + 1) * chunk)
        grads_2[here, :] = query_grad_2
        summ_2[here, :] = summary_2
        wide_s = dot(query_grad_2, bd_nn[...])
        summary_grad = wide_s[:, :LANES] + wide_s[:, LANES:]
        spread_grad = summary_grad * summary * (1.0 - summary)
        spread_grad += back[i * chunk : (i + 1) * chunk, :]
        eg[piece] = embed_grad.reshape(step, LANES, LANES)
        mix[here, :] = jnp.where(lax.rem(lane, lats) < lats // 2, logit_same, logit_other)
        for j in range(step):
            put(3, i * step + j, spread_grad[j * LANES : (j + 1) * LANES, :])
    halo_start(3)

    disc_total = jnp.zeros((2 * LANES, 2 * LANES), F32)
    for i in range(CHUNKS):
        here = slice(i * chunk, (i + 1) * chunk)
        disc_total += dot(grads_2[here, :], summ_2[here, :], 0, 0)
    quarter = (disc_total[:LANES, :LANES] + disc_total[LANES:, :LANES]) + (
        disc_total[:LANES, LANES:] + disc_total[LANES:, LANES:]
    )
    disc_src[...] = quarter[:lats, :] + swap(quarter[lats:, :])

    def part_of(index):
        return pl.ds(pl.multiple_of(index * part, 8), part)

    def disc_1(k):
        other = lax.rem(c + k, n_col)
        return pltpu.make_async_remote_copy(
            src_ref=disc_src.at[part_of(other)],
            dst_ref=disc_a.at[c],
            send_sem=ds_sem.at[0],
            recv_sem=dr_sem.at[0],
            device_id=(r, other),
            device_id_type=MESH,
        )

    disc_a[c] = disc_src[part_of(c), :]
    peers(n_col, disc_1)

    for i in range(rows):
        flipped = mix[i * LANES : (i + 1) * LANES, :].T
        for k in range(4):
            at = k * (lats // 2)
            log_out[k, i : i + 1, :] = flipped[at : at + 1, :]
    outs[4].start()
    rs1_finish(0)
    rs2_start(0)

    halo_take(3)

    def to_latent_grad(i, value):
        z = lat[i]
        slope = jnp.where(z > 0, 1.0, jnp.exp(jnp.minimum(z, 0.0)))
        put(4, i, (eg[i] + value) * slope)

    stencil(3, to_latent_grad)
    halo_start(4)

    drain(disc_a, n_col, ds_sem.at[0], dr_sem.at[0])
    disc_bsrc[...] = jnp.sum(disc_a[...], axis=0)

    def disc_2(k):
        other = lax.rem(r + k, n_row)
        return pltpu.make_async_remote_copy(
            src_ref=disc_bsrc,
            dst_ref=disc_b.at[r],
            send_sem=ds_sem.at[1],
            recv_sem=dr_sem.at[1],
            device_id=(other, c),
            device_id_type=MESH,
        )

    disc_b[r] = disc_bsrc[...]
    peers(n_row, disc_2)
    dec_sum[...] = rs2_finish(0)

    halo_take(4)

    def to_proj_grad(i, value):
        pg_low[i * LANES : (i + 1) * LANES, :] = value.astype(BF16)

    stencil(4, to_proj_grad)

    returned = dot(recv_pick_t[...], pg_low[...])
    ex_src[1] = returned.astype(BF16).reshape(n_dev, portion, LANES)
    ex_start(1)
    for i in range(rows):
        here = slice(i * LANES, (i + 1) * LANES)
        flipped = pg_low[here, :].astype(F32).T
        stage[:, i, :] = flipped
        own[:, here] = flipped[:lats, :].astype(BF16)
    pg_out[...] = stage[...].astype(BF16)
    outs[5].start()

    drain(disc_b, n_row, ds_sem.at[1], dr_sem.at[1])
    disc_full[c] = jnp.sum(disc_b[...], axis=0)

    def disc_3(k):
        other = lax.rem(c + k, n_col)
        return pltpu.make_async_remote_copy(
            src_ref=disc_full.at[c],
            dst_ref=disc_full.at[c],
            send_sem=ds_sem.at[2],
            recv_sem=dr_sem.at[2],
            device_id=(r, other),
            device_id_type=MESH,
        )

    peers(n_col, disc_3)

    for turn in range(ROUNDS):
        halo_finish(turn)

    lt[0:lats, :] = own[...]
    home = ex_wait(1)
    flipped = jnp.concatenate(
        [home[i * LANES : (i + 1) * LANES, :].astype(F32).T[lats:, :] for i in range(rows)], axis=1
    ).astype(BF16)
    lt[lats:, :] = dot(flipped, send_pick[...]).astype(BF16)

    def encoder_part(where):
        value = dot(lt[...], x[:, where])
        return value[:lats, :] + value[lats:, :]

    rs1_run(1, encoder_part)

    drain(disc_full, n_col, ds_sem.at[2], dr_sem.at[2])
    disc_grad = disc_full[...].reshape(lats, LANES)[:, :lats]
    disc_mean = jnp.sum(disc_grad * disc_grad) / (lats * lats)
    disc_out[...] = disc_grad * lax.rsqrt(disc_mean + 1e-06)
    outs[2].start()

    rs1_finish(1)
    rs2_start(1)
    enc_sum = rs2_finish(1)

    def squares(value):
        return jnp.broadcast_to(jnp.sum(value * value), (8, LANES))

    norm_src[0] = squares(enc_sum)
    norm_src[1] = squares(dec_sum[...])

    def norm_1(k):
        other = lax.rem(r + k, n_row)
        return pltpu.make_async_remote_copy(
            src_ref=norm_src,
            dst_ref=norm_a.at[r],
            send_sem=ns_sem.at[0],
            recv_sem=nr_sem.at[0],
            device_id=(other, c),
            device_id_type=MESH,
        )

    norm_a[r] = norm_src[...]
    peers(n_row, norm_1)
    drain(norm_a, n_row, ns_sem.at[0], nr_sem.at[0])
    norm_bsrc[...] = jnp.sum(norm_a[...], axis=0)

    def norm_2(k):
        other = lax.rem(c + k, n_col)
        return pltpu.make_async_remote_copy(
            src_ref=norm_bsrc,
            dst_ref=norm_b.at[c],
            send_sem=ns_sem.at[1],
            recv_sem=nr_sem.at[1],
            device_id=(r, other),
            device_id_type=MESH,
        )

    norm_b[c] = norm_bsrc[...]
    peers(n_col, norm_2)
    drain(norm_b, n_col, ns_sem.at[1], nr_sem.at[1])
    totals = jnp.sum(norm_b[...], axis=0)
    entries = genes * lats
    enc_out[...] = enc_sum[:, :lats] * lax.rsqrt(totals[0, 0:1, 0:1] / entries + 1e-06)
    dec_out[...] = dec_sum[:, :lats] * lax.rsqrt(totals[1, 0:1, 0:1] / entries + 1e-06)
    outs[0].start()
    outs[1].start()
    for out in outs:
        out.wait()


def hand_on(*refs):
    count = (len(refs) - 2) // 3
    sources, targets, held = (refs[k * count : (k + 1) * count] for k in range(3))
    come, go = refs[3 * count :]
    ins = [pltpu.make_async_copy(sources[i], held[i], come.at[i]) for i in range(count)]
    outs = [pltpu.make_async_copy(held[i], targets[i], go.at[i]) for i in range(count)]
    for copy in ins:
        copy.start()
    for i in range(count):
        ins[i].wait()
        outs[i].start()
    for copy in outs:
        copy.wait()


def per_device(features, enc_weight, dec_weight, disc_weight, send_order, recv_order):
    tile_rows, tile_cols, genes = features.shape
    lats = enc_weight.shape[1]
    bins = tile_rows * tile_cols
    n_row = lax.axis_size("row")
    n_col = lax.axis_size("col")
    n_dev = n_row * n_col
    n_group = n_row // 2
    per_dev = genes // n_dev
    span = genes // n_group
    part = lats // n_col
    portion = bins // n_dev
    field = (tile_rows, LANES, LANES)
    dma = pltpu.SemaphoreType.DMA
    vmem = pltpu.VMEM
    shape = jax.ShapeDtypeStruct
    out_shape = [
        shape((per_dev, lats), F32),
        shape((per_dev, lats), F32),
        shape((lats, lats), F32),
        shape((lats, tile_rows, tile_cols), F32),
        shape((4, tile_rows, tile_cols), F32),
        shape((2 * lats, tile_rows, tile_cols), BF16),
    ]
    scratch = [
        *(vmem(one.shape, one.dtype) for one in out_shape),
        vmem((bins, genes), BF16),
        vmem((lats, lats), F32),
        vmem((2, tile_rows, LANES), jnp.int32),
        vmem((2 * lats, genes), BF16),
        vmem((2 * lats, genes), BF16),
        vmem((LANES, LANES), BF16),
        vmem((2 * LANES, 2 * LANES), BF16),
        vmem((2 * LANES, 2 * LANES), BF16),
        vmem((bins, bins), BF16),
        vmem((bins, bins), BF16),
        vmem((bins, bins), BF16),
        vmem((bins, LANES), F32),
        vmem((bins, LANES), BF16),
        vmem((2, n_dev, portion, LANES), BF16),
        vmem((2, n_dev, portion, LANES), BF16),
        vmem((2, tile_rows + 2 * RADIUS, LANES + 2 * SIDE, LANES), F32),
        vmem((tile_rows, LANES + 2 * SIDE, LANES), F32),
        vmem((ROUNDS,) + field, BF16),
        vmem((ROUNDS, 2, RADIUS, LANES, LANES), BF16),
        vmem((ROUNDS, 2, tile_rows, EDGE, LANES), BF16),
        vmem((ROUNDS, 4, RADIUS, EDGE, LANES), BF16),
        vmem((len(PACKED), 2, RADIUS, LANES // 2, LANES), BF16),
        vmem((len(PACKED), 2, RADIUS, LANES // 2, LANES), BF16),
        vmem(field, F32),
        vmem(field, F32),
        vmem(field, F32),
        vmem(field, F32),
        vmem((bins, LANES), BF16),
        vmem((bins, LANES), F32),
        vmem((bins, 2 * LANES), BF16),
        vmem((bins, 2 * LANES), BF16),
        vmem((bins, LANES), F32),
        vmem(field, F32),
        vmem((bins, LANES), BF16),
        vmem((LANES, bins), BF16),
        vmem((lats, bins), BF16),
        vmem((2, n_group, lats, span), BF16),
        vmem((2, n_group, lats, span), BF16),
        vmem((2, span, LANES), F32),
        vmem((2, 2 * n_col, per_dev, LANES), F32),
        vmem((lats, LANES), F32),
        vmem((n_col, part, LANES), F32),
        vmem((part, LANES), F32),
        vmem((n_row, part, LANES), F32),
        vmem((n_col, part, LANES), F32),
        vmem((2, 8, LANES), F32),
        vmem((n_row, 2, 8, LANES), F32),
        vmem((2, 8, LANES), F32),
        vmem((n_col, 2, 8, LANES), F32),
        vmem((LANES, tile_rows, LANES), F32),
        vmem((per_dev, LANES), F32),
        dma((7,)),
        dma((tile_rows,)),
        dma((ROUNDS, 8)),
        dma((ROUNDS, 8)),
        dma((2,)),
        dma((2,)),
        dma((2,)),
        dma((2,)),
        dma((2,)),
        dma((2,)),
        dma((3,)),
        dma((3,)),
        dma((2,)),
        dma((2,)),
        pltpu.SemaphoreType.REGULAR,
        dma((6,)),
    ]
    anywhere = [pl.BlockSpec(memory_space=pl.ANY)] * 6
    results = pl.pallas_call(
        functools.partial(kernel, n_row, n_col),
        out_shape=out_shape,
        in_specs=anywhere,
        out_specs=anywhere,
        scratch_shapes=scratch,
        compiler_params=pltpu.CompilerParams(
            collective_id=0, has_side_effects=True, vmem_limit_bytes=56 * 1024 * 1024
        ),
    )(
        features.reshape(bins, genes),
        enc_weight.T,
        dec_weight.T,
        disc_weight,
        send_order.reshape(tile_rows, LANES),
        recv_order.reshape(tile_rows, LANES),
    )
    *others, grads = pl.pallas_call(
        hand_on,
        out_shape=out_shape,
        in_specs=anywhere,
        out_specs=anywhere,
        scratch_shapes=[*(vmem(one.shape, one.dtype) for one in out_shape), dma((6,)), dma((6,))],
    )(*results)
    return (*others, grads.reshape(2, lats, tile_rows, tile_cols))


def solution(mesh):
    in_specs = (P("row", "col", None), P(), P(), P(), P("row", "col", None), P("row", "col", None))
    out_specs = (
        P(("row", "col"), None),
        P(("row", "col"), None),
        P(),
        P(None, "row", "col"),
        P(None, "row", "col"),
        P(None, None, "row", "col"),
    )
    return jax.shard_map(
        per_device, mesh=mesh, in_specs=in_specs, out_specs=out_specs, check_vma=False
    )
```

time: 1130 us -> 94.2 us (0.08)
  waiting for transfers between devices: 903 us -> 0 us
  Pallas kernels: 0 us -> 93.3 us
  blocking collectives: 77.1 us -> 0 us
  starting transfers between devices: 58.7 us -> 0 us
  local copies, waits for them, and re-layouts: 37.3 us -> 0 us
  matrix products: 24.7 us -> 0 us
  between operations: 16.7 us -> 0.8 us
  other arithmetic: 15.8 us -> 0 us
    unnamed x4 -> x0, waiting for transfers between devices: 774 us -> none
    pallas_call x0 -> x2, Pallas kernels: none -> 93.3 us  [the longest x1 91.4 us: per_device(): pl.pallas_call(functools.partial(kernel, n_row, n_col), out_shape=out_sha...]
    psum x1 -> x0, blocking collectives: 77.1 us -> none  [per_device(): enc_total, dec_total = lax.psum((enc_square, dec_square), ('row', 'col'))]
    all_to_all x1 -> x0, waiting for transfers between devices: 71.6 us -> none  [per_device(): lax.all_to_all(outgoing, ('row', 'col'), split_axis=0, concat_axis=0, til...]
    ppermute x16 -> x0, waiting for transfers between devices: 57.3 us -> none  [the longest x8 35.2 us: padded_2(): after = lax.ppermute(leading, axis, down)]
    ppermute x16 -> x0, starting transfers between devices: 46.7 us -> none  [the longest x8 32 us: padded_2(): before = lax.ppermute(last, axis, up)]
    gather x2 -> x0, local copies, waits for them, and re-layouts: 31.6 us -> none  [the longest x1 15.8 us: per_device(): outgoing = flat_bins[sending].reshape(devices, portion, gene_count)]
    dot_general x10 -> x0, matrix products: 24.7 us -> none  [the longest x1 5.78 us: per_device(): lax.dot_general(rec_slope, spread_low, FIRST_WITH_SECOND, preferred_eleme...]
  transfers between devices with their start and end apart: 19 -> 0, of which waited for: 15 -> 0; matrix products, arithmetic and copies ran while one was open for 1% -> 0% of each run, Pallas kernels for 0% -> 0%
where the time goes in v1:
time: 94.2 us; the launch traced here: 94.1 us
  Pallas kernels  93.3 us (99%)
    pallas_call x1, Pallas kernels, per_device(): pl.pallas_call(functools.partial(kernel, n_row, n_col), out_shape=out_sha...  91.4 us
    pallas_call x1, Pallas kernels, per_device(): pl.pallas_call(hand_on, out_shape=out_shape, in_specs=anywhere, out_specs...  1.91 us

profile of v1, /device:TPU:1, one launch (start us, length us, event | category | flops | bytes accessed | tf_op | source)
XLA Modules:
  0.0 94.1 jit_solution(3352583354197353477)
XLA Ops:
  0.6 91.4 %shard_map.109 = (f32[24,64]{1,0:T(8,128)}, f32[24,64]{1,0:T(8,128)}, f32[64,64]{1,0:T(8,128)}, f32[64,8,128]{2,1,0:T(8,128)}, f32[4,8,128]{2,1,0:T(8,128)}, /*index=5*/bf16[128,8,128]{2,1,0:T(8,128)(2,1)}) custom-call(bf16[1024,3072]{1,0:T(8,128)(2,1)} %bitcast.6, bf16[64,3072]{1,0:T(8,128)(2,1)} %bitcast.7, bf16[64,3072]{1,0:T(8,128)(2,1)} %bitcast.8, ...), custom_call_target="tpu_custom_call" | custom-call | tf_op jit(solution)/shard_map/pallas_call | solution.py:893
  92.0 1.9 %shard_map.110 = (f32[24,64]{1,0:T(8,128)}, f32[24,64]{1,0:T(8,128)}, f32[64,64]{1,0:T(8,128)}, f32[64,8,128]{2,1,0:T(8,128)}, f32[4,8,128]{2,1,0:T(8,128)}, /*index=5*/bf16[128,8,128]{2,1,0:T(8,128)(2,1)}) custom-call(f32[24,64]{1,0:T(8,128)} %get-tuple-element.18.refs_0_, f32[24,64]{1,0:T(8,128)} %get-tuple-element.19.refs_1_, ...), custom_call_target="tpu_custom_call" | custom-call | tf_op jit(solution)/shard_map/pallas_call | solution.py:910

commit v2 on v1

--- a/solution.py
+++ b/solution.py
@@ -31,6 +31,14 @@
 
 def dot(a, b, ca=1, cb=0):
     return lax.dot_general(a, b, (((ca,), (cb,)), ((), ())), preferred_element_type=F32)
+
+
+def each(count, body):
+    def step(i, carry):
+        body(i)
+        return carry
+
+    lax.fori_loop(0, count, step, 0)
 
 
 def split_2(value):
@@ -75,6 +83,7 @@
     xp_low,
     ex_src,
     ex_dst,
+    low_in,
     pads,
     tmp,
     hsrc,
@@ -107,8 +116,7 @@
     disc_full,
     norm_src,
     norm_a,
-    norm_bsrc,
-    norm_b,
+    by_gene,
     stage,
     dec_sum,
     load_sem,
@@ -135,9 +143,9 @@
     portion = bins // n_dev
     n_group = n_row // 2
     n_pair = n_group // 2
+    width = 2 * LANES
     per_dev = genes // n_dev
     span = genes // n_group
-    per_group = 2 * n_col
     part = lats // n_col
     slope_scale = 2.0 * RECON_WEIGHT / genes
     tap = stencil_taps()
@@ -246,21 +254,30 @@
 
     def stencil(turn, then):
         pad = pads.at[turn % 2]
-        for t in range(0, LANES + 2 * SIDE, SIDE):
-            block = pad[:, t : t + SIDE, :]
+
+        def down(t):
+            at = pl.ds(pl.multiple_of(t * SIDE, SIDE), SIDE)
+            block = pad[:, at, :]
             across = tap[RADIUS] * block[RADIUS : RADIUS + rows]
             for k in range(1, RADIUS + 1):
                 across += tap[RADIUS + k] * (
                     block[RADIUS - k : RADIUS - k + rows] + block[RADIUS + k : RADIUS + k + rows]
                 )
-            tmp[:, t : t + SIDE, :] = across
-        for i in range(rows):
+            tmp[:, at, :] = across
+
+        def along(i):
             total = tap[RADIUS] * tmp[i, SIDE : SIDE + LANES, :]
             for k in range(1, RADIUS + 1):
                 total += tap[RADIUS + k] * (
                     tmp[i, SIDE - k : SIDE - k + LANES, :] + tmp[i, SIDE + k : SIDE + k + LANES, :]
                 )
             then(i, total)
+
+        each(LANES // SIDE + 2, down)
+        each(rows, along)
+
+    def bins_of(i, size=LANES):
+        return pl.ds(pl.multiple_of(i * size, size), size)
 
     def put(turn, i, value):
         pads[turn % 2, i + RADIUS, SIDE : SIDE + LANES, :] = value
@@ -275,9 +292,13 @@
             packed = jnp.where(first, front, swap(rear)).astype(BF16)
         else:
             packed = jnp.where(first, swap(front), rear).astype(BF16)
-        if i < RADIUS:
+
+        @pl.when(i < RADIUS)
+        def _():
             pack_src[PACKED[turn], 0, i] = packed
-        if i >= rows - RADIUS:
+
+        @pl.when(i >= rows - RADIUS)
+        def _():
             pack_src[PACKED[turn], 1, i - (rows - RADIUS)] = packed
 
     loads = [
@@ -296,12 +317,10 @@
     ]
     for load in loads[:4]:
         load.start()
-    feats = []
     for i in range(rows):
         piece = pl.ds(i * LANES, LANES)
         copy = pltpu.make_async_copy(feat_hbm.at[piece], x.at[piece], feat_sem.at[i])
         copy.start()
-        feats.append(copy)
     for load in loads[4:]:
         load.start()
 
@@ -321,14 +340,16 @@
     lax.fori_loop(1, n_col, greet_col, 0)
 
     def build_send():
-        for a in range(rows):
-            line = orders[0, a : a + 1, :].astype(F32)
+        def body(a):
+            line = orders[0, pl.ds(a, 1), :].astype(F32)
             column = jnp.broadcast_to(line, (LANES, LANES)).T
             for t in range(rows):
                 index = (lane + t * LANES).astype(F32)
-                send_pick[a * LANES : (a + 1) * LANES, t * LANES : (t + 1) * LANES] = jnp.where(
+                send_pick[bins_of(a), t * LANES : (t + 1) * LANES] = jnp.where(
                     column == index, 1.0, 0.0
                 ).astype(BF16)
+
+        each(rows, body)
 
     def build_recv():
         def body(a, carry):
@@ -386,7 +407,6 @@
         drain(ex_dst.at[which], n_dev, as_sem.at[which], ar_sem.at[which])
         return ex_dst[which].reshape(bins, LANES)
 
-    rs2_src[...] = jnp.zeros_like(rs2_src)
     loads[0].wait()
     loads[1].wait()
     build_send()
@@ -404,16 +424,6 @@
     loads[2].wait()
     loads[3].wait()
 
-    for i in range(2):
-        for k in range(rows // 2):
-            feats[i * (rows // 2) + k].wait()
-        piece = slice(i * (bins // 2), (i + 1) * (bins // 2))
-        acc = dot(x[piece, :], wcat[...], 1, 1)
-        xp[piece, :] = acc
-        xp_low[piece, :] = acc.astype(BF16)
-    outgoing = dot(send_pick[...], xp_low[...])
-    ex_src[0] = outgoing.astype(BF16).reshape(n_dev, portion, LANES)
-
     pl.semaphore_wait(barrier, n_row + n_col - 2)
 
     def greet_meet(k, carry):
@@ -422,13 +432,31 @@
         return carry
 
     lax.fori_loop(1, n_col, greet_meet, 0)
+    def project(i):
+        for k in range(rows // CHUNKS):
+            at = i * (rows // CHUNKS) + k
+            pltpu.make_async_copy(
+                feat_hbm.at[bins_of(at)], x.at[bins_of(at)], feat_sem.at[at]
+            ).wait()
+        acc = dot(x[bins_of(i, chunk), :], wcat[...], 1, 1)
+        xp[bins_of(i, chunk), :] = acc
+        xp_low[bins_of(i, chunk), :] = acc.astype(BF16)
+
+    each(CHUNKS, project)
+
+    def pick_out(i):
+        value = dot(send_pick[bins_of(i, chunk), :], xp_low[...])
+        ex_src[0, pl.ds(i * (n_dev // CHUNKS), n_dev // CHUNKS)] = value.astype(BF16).reshape(
+            n_dev // CHUNKS, portion, LANES
+        )
+
+    each(CHUNKS, pick_out)
+
     pl.semaphore_wait(meet_sem, n_col - 1)
 
     ex_start(0)
 
-    for i in range(rows):
-        piece = slice(i * LANES, (i + 1) * LANES)
-        put(0, i, swap(xp_low[piece, :].astype(F32)))
+    each(rows, lambda i: put(0, i, swap(xp_low[bins_of(i), :].astype(F32))))
     halo_start(0)
     build_recv()
     def elu(value):
@@ -441,9 +469,16 @@
     halo_take(0)
     stencil(0, first_latent)
 
-    scrambled = dot(recv_pick[...], ex_wait(0))
-    for i in range(rows):
-        put(1, i, jnp.where(first, emb[i], scrambled[i * LANES : (i + 1) * LANES, :]))
+    arrived = ex_wait(0)
+    low_in[...] = arrived
+
+    def pick_in(i):
+        value = dot(recv_pick[bins_of(i, chunk), :], low_in[...])
+        for k in range(rows // CHUNKS):
+            at = i * (rows // CHUNKS) + k
+            put(1, at, jnp.where(first, emb[at], value[k * LANES : (k + 1) * LANES, :]))
+
+    each(CHUNKS, pick_in)
     halo_start(1)
     build_recv_t()
     gram = dot(wcat[0:lats, :], wcat[0:lats, :], 1, 1)
@@ -463,89 +498,89 @@
     halo_take(1)
     stencil(1, first_spread)
     halo_start(2)
-    for i in range(rows):
+
+    def after_spread(i):
         value = spread[i]
-        here = slice(i * LANES, (i + 1) * LANES)
+        here = bins_of(i)
         low = value.astype(BF16).astype(F32)
         summ[i] = jax.nn.sigmoid(value)
         s_low[here, :] = jnp.where(first, low, swap(low)).astype(BF16)
         lt[0:lats, here] = low.T[0:lats, :].astype(BF16)
 
+    each(rows, after_spread)
+
     back[...] = slope_scale * (
         dot(s_low[...], gram2[...]) - jnp.where(first, xp[...], 0.0)
     )
 
-    def rs1_copy(which, group):
+    def rs1_copy(which, target):
         return pltpu.make_async_remote_copy(
-            src_ref=rs1_src.at[which, group],
-            dst_ref=rs1_dst.at[which, my_group],
+            src_ref=rs1_src.at[which, target],
+            dst_ref=rs1_dst.at[which, r],
             send_sem=r1s_sem.at[which],
             recv_sem=r1r_sem.at[which],
-            device_id=(2 * group + lax.rem(r, 2), c),
+            device_id=(target, c),
             device_id_type=MESH,
         )
 
     def rs1_run(which, product):
-        for k in range(n_pair):
+        def body(k):
             pair = lax.rem(my_group // 2 + 1 + k, n_pair)
-            where = pl.ds(pl.multiple_of(pair * (2 * span), LANES), 2 * span)
+            where = bins_of(pair, 2 * span)
             value = product(where).astype(BF16)
-            for j in range(2):
-                rs1_src[which, 2 * pair + j] = value[:, j * span : (j + 1) * span]
-            if k < n_pair - 1:
-                for j in range(2):
-                    rs1_copy(which, 2 * pair + j).start()
-            else:
-                rs1_copy(which, my_group + 1 - 2 * lax.rem(my_group, 2)).start()
+            for j in range(4):
+                at = (j // 2) * span + (j % 2) * LANES
+                rs1_src[which, 4 * pair + j] = value[:, at : at + width]
+            for j in range(4):
+
+                @pl.when(4 * pair + j != r)
+                def _():
+                    rs1_copy(which, 4 * pair + j).start()
+
+        each(n_pair, body)
 
     def rs1_finish(which):
-        seven = rs1_dst.at[which, pl.ds(0, n_group - 1)]
-        pltpu.make_async_copy(seven, seven, r1r_sem.at[which]).wait()
-        pltpu.make_async_copy(seven, seven, r1s_sem.at[which]).wait()
-        rs1_dst[which, my_group] = rs1_src[which, my_group]
+        drain(rs1_dst.at[which], n_row, r1s_sem.at[which], r1r_sem.at[which])
+        rs1_dst[which, r] = rs1_src[which, r]
         total = rs1_dst[which, 0].astype(F32)
-        for group in range(1, n_group):
-            total += rs1_dst[which, group].astype(F32)
-        for k in range(span // LANES):
-            rs2_src[which, k * LANES : (k + 1) * LANES, 0:lats] = total[
-                :, k * LANES : (k + 1) * LANES
-            ].T
-
-    mine = lax.rem(r, 2) * n_col + c
-
-    def gene_part(index):
-        return pl.ds(pl.multiple_of(index * per_dev, 8), per_dev)
+        for k in range(1, n_row):
+            total += rs1_dst[which, k].astype(F32)
+        rs2_src[which] = total.astype(BF16)
+
+    def rs2_copy(which, k):
+        other = lax.rem(c + k, n_col)
+        return pltpu.make_async_remote_copy(
+            src_ref=rs2_src.at[which],
+            dst_ref=rs2_dst.at[which, c],
+            send_sem=r2s_sem.at[which],
+            recv_sem=r2r_sem.at[which],
+            device_id=(r, other),
+            device_id_type=MESH,
+        )
 
     def rs2_start(which):
-        def body(k, carry):
-            other = lax.rem(mine + k, per_group)
-            pltpu.make_async_remote_copy(
-                src_ref=rs2_src.at[which, gene_part(other)],
-                dst_ref=rs2_dst.at[which, mine],
-                send_sem=r2s_sem.at[which],
-                recv_sem=r2r_sem.at[which],
-                device_id=((r // 2) * 2 + other // n_col, lax.rem(other, n_col)),
-                device_id_type=MESH,
-            ).start()
-            return carry
-
-        rs2_dst[which, mine] = rs2_src[which, gene_part(mine), :]
-        lax.fori_loop(1, per_group, body, 0)
+        peers(n_col, functools.partial(rs2_copy, which))
+        rs2_dst[which, c] = rs2_src[which]
 
     def rs2_finish(which):
-        most = rs2_dst.at[which, pl.ds(0, per_group - 1)]
-        pltpu.make_async_copy(most, most, r2r_sem.at[which]).wait()
-        pltpu.make_async_copy(most, most, r2s_sem.at[which]).wait()
-        total = rs2_dst[which, 0]
-        for k in range(1, per_group):
-            total += rs2_dst[which, k]
-        return jnp.where(first, total, 0.0)
-
-    loads[4].wait()
-    loads[5].wait()
+        drain(rs2_dst.at[which], n_col, r2s_sem.at[which], r2r_sem.at[which])
+        total = rs2_dst[which, 0].astype(F32)
+        for k in range(1, n_col):
+            total += rs2_dst[which, k].astype(F32)
+        begin = lax.rem(r, 2) * (width - span // 2)
+        gene = lax.broadcasted_iota(jnp.int32, (1, width), 1) - begin
+        own_genes = jnp.where((gene >= 0) & (gene < span // 2), total, 0.0)
+        for k in range(width // LANES):
+            by_gene[k * LANES : (k + 1) * LANES, :] = total[:, k * LANES : (k + 1) * LANES].T
+        mine = by_gene[pl.ds(pl.multiple_of(begin + c * per_dev, 8), per_dev), :]
+        norm_src[which] = jnp.broadcast_to(jnp.sum(own_genes * own_genes), (8, LANES))
+        return mine
+
     square = dot(lt[0:lats, :], s_low[...])
     square_high = square.astype(BF16).astype(F32)
     square2 = jnp.where(first, square_high, square - square_high).astype(BF16)
+    loads[4].wait()
+    loads[5].wait()
     rs1_run(
         0,
         lambda where: slope_scale
@@ -583,8 +618,10 @@
     half_sum2 = jnp.concatenate([half_sum, half_sum], axis=0)
 
     step = rows // CHUNKS
-    for i in range(CHUNKS):
-        piece = slice(i * step, (i + 1) * step)
+
+    def contrast(i):
+        piece = pl.ds(i * step, step)
+        here = bins_of(i, chunk)
         summary = summ[piece].reshape(chunk, LANES)
         embedded = emb[piece].reshape(chunk, LANES)
         swapped = swap(embedded)
@@ -598,23 +635,27 @@
         embed_grad = grad_same * queries + swap(grad_other * queries)
         query_grad = grad_same * embedded + grad_other * swapped
         query_grad_2 = split_2(query_grad)
-        here = slice(i * chunk, (i + 1) * chunk)
         grads_2[here, :] = query_grad_2
         summ_2[here, :] = summary_2
         wide_s = dot(query_grad_2, bd_nn[...])
         summary_grad = wide_s[:, :LANES] + wide_s[:, LANES:]
         spread_grad = summary_grad * summary * (1.0 - summary)
-        spread_grad += back[i * chunk : (i + 1) * chunk, :]
+        spread_grad += back[here, :]
         eg[piece] = embed_grad.reshape(step, LANES, LANES)
         mix[here, :] = jnp.where(lax.rem(lane, lats) < lats // 2, logit_same, logit_other)
         for j in range(step):
             put(3, i * step + j, spread_grad[j * LANES : (j + 1) * LANES, :])
+
+    each(CHUNKS, contrast)
     halo_start(3)
 
-    disc_total = jnp.zeros((2 * LANES, 2 * LANES), F32)
-    for i in range(CHUNKS):
-        here = slice(i * chunk, (i + 1) * chunk)
-        disc_total += dot(grads_2[here, :], summ_2[here, :], 0, 0)
+    def disc_step(i, total):
+        here = bins_of(i, chunk)
+        return total + dot(grads_2[here, :], summ_2[here, :], 0, 0)
+
+    disc_total = lax.fori_loop(
+        0, CHUNKS, disc_step, jnp.zeros((2 * LANES, 2 * LANES), F32)
+    )
     quarter = (disc_total[:LANES, :LANES] + disc_total[LANES:, :LANES]) + (
         disc_total[:LANES, LANES:] + disc_total[LANES:, LANES:]
     )
@@ -677,12 +718,17 @@
     halo_take(4)
 
     def to_proj_grad(i, value):
-        pg_low[i * LANES : (i + 1) * LANES, :] = value.astype(BF16)
+        pg_low[bins_of(i), :] = value.astype(BF16)
 
     stencil(4, to_proj_grad)
 
-    returned = dot(recv_pick_t[...], pg_low[...])
-    ex_src[1] = returned.astype(BF16).reshape(n_dev, portion, LANES)
+    def pick_back(i):
+        value = dot(recv_pick_t[bins_of(i, chunk), :], pg_low[...])
+        ex_src[1, pl.ds(i * (n_dev // CHUNKS), n_dev // CHUNKS)] = value.astype(BF16).reshape(
+            n_dev // CHUNKS, portion, LANES
+        )
+
+    each(CHUNKS, pick_back)
     ex_start(1)
     for i in range(rows):
         here = slice(i * LANES, (i + 1) * LANES)
@@ -734,12 +780,6 @@
     rs2_start(1)
     enc_sum = rs2_finish(1)
 
-    def squares(value):
-        return jnp.broadcast_to(jnp.sum(value * value), (8, LANES))
-
-    norm_src[0] = squares(enc_sum)
-    norm_src[1] = squares(dec_sum[...])
-
     def norm_1(k):
         other = lax.rem(r + k, n_row)
         return pltpu.make_async_remote_copy(
@@ -754,26 +794,10 @@
     norm_a[r] = norm_src[...]
     peers(n_row, norm_1)
     drain(norm_a, n_row, ns_sem.at[0], nr_sem.at[0])
-    norm_bsrc[...] = jnp.sum(norm_a[...], axis=0)
-
-    def norm_2(k):
-        other = lax.rem(c + k, n_col)
-        return pltpu.make_async_remote_copy(
-            src_ref=norm_bsrc,
-            dst_ref=norm_b.at[c],
-            send_sem=ns_sem.at[1],
-            recv_sem=nr_sem.at[1],
-            device_id=(r, other),
-            device_id_type=MESH,
-        )
-
-    norm_b[c] = norm_bsrc[...]
-    peers(n_col, norm_2)
-    drain(norm_b, n_col, ns_sem.at[1], nr_sem.at[1])
-    totals = jnp.sum(norm_b[...], axis=0)
+    totals = jnp.sum(norm_a[...], axis=0)
     entries = genes * lats
-    enc_out[...] = enc_sum[:, :lats] * lax.rsqrt(totals[0, 0:1, 0:1] / entries + 1e-06)
-    dec_out[...] = dec_sum[:, :lats] * lax.rsqrt(totals[1, 0:1, 0:1] / entries + 1e-06)
+    enc_out[...] = enc_sum * lax.rsqrt(totals[1, 0:1, 0:1] / entries + 1e-06)
+    dec_out[...] = dec_sum[...] * lax.rsqrt(totals[0, 0:1, 0:1] / entries + 1e-06)
     outs[0].start()
     outs[1].start()
     for out in outs:
@@ -836,6 +860,7 @@
         vmem((bins, LANES), BF16),
         vmem((2, n_dev, portion, LANES), BF16),
         vmem((2, n_dev, portion, LANES), BF16),
+        vmem((bins, LANES), BF16),
         vmem((2, tile_rows + 2 * RADIUS, LANES + 2 * SIDE, LANES), F32),
         vmem((tile_rows, LANES + 2 * SIDE, LANES), F32),
         vmem((ROUNDS,) + field, BF16),
@@ -857,10 +882,10 @@
         vmem((bins, LANES), BF16),
         vmem((LANES, bins), BF16),
         vmem((lats, bins), BF16),
-        vmem((2, n_group, lats, span), BF16),
-        vmem((2, n_group, lats, span), BF16),
-        vmem((2, span, LANES), F32),
-        vmem((2, 2 * n_col, per_dev, LANES), F32),
+        vmem((2, n_row, lats, 2 * LANES), BF16),
+        vmem((2, n_row, lats, 2 * LANES), BF16),
+        vmem((2, lats, 2 * LANES), BF16),
+        vmem((2, n_col, lats, 2 * LANES), BF16),
         vmem((lats, LANES), F32),
         vmem((n_col, part, LANES), F32),
         vmem((part, LANES), F32),
@@ -868,10 +893,9 @@
         vmem((n_col, part, LANES), F32),
         vmem((2, 8, LANES), F32),
         vmem((n_row, 2, 8, LANES), F32),
-        vmem((2, 8, LANES), F32),
-        vmem((n_col, 2, 8, LANES), F32),
+        vmem((2 * LANES, lats), F32),
         vmem((LANES, tile_rows, LANES), F32),
-        vmem((per_dev, LANES), F32),
+        vmem((per_dev, lats), F32),
         dma((7,)),
         dma((tile_rows,)),
         dma((ROUNDS, 8)),
@@ -884,8 +908,8 @@
         dma((2,)),
         dma((3,)),
         dma((3,)),
-        dma((2,)),
-        dma((2,)),
+        dma((1,)),
+        dma((1,)),
         pltpu.SemaphoreType.REGULAR,
         dma((6,)),
     ]

time: 94.2 us -> 91.5 us (0.971)
  Pallas kernels: 93.3 us -> 90.7 us
    pallas_call x1, Pallas kernels: 91.4 us -> 88.8 us  [per_device(): pl.pallas_call(functools.partial(kernel, n_row, n_col), out_shape=out_sha...]
where the time goes in v2:
time: 91.5 us; the launch traced here: 91.3 us
  Pallas kernels  90.7 us (99%)
    pallas_call x1, Pallas kernels, per_device(): pl.pallas_call(functools.partial(kernel, n_row, n_col), out_shape=out_sha...  88.8 us
    pallas_call x1, Pallas kernels, per_device(): pl.pallas_call(hand_on, out_shape=out_shape, in_specs=anywhere, out_specs...  1.91 us

profile of v2, /device:TPU:1, one launch (start us, length us, event | category | flops | bytes accessed | tf_op | source)
XLA Modules:
  0.0 91.3 jit_solution(9153232182544855548)
XLA Ops:
  0.6 88.8 %shard_map.109 = (f32[24,64]{1,0:T(8,128)}, f32[24,64]{1,0:T(8,128)}, f32[64,64]{1,0:T(8,128)}, f32[64,8,128]{2,1,0:T(8,128)}, f32[4,8,128]{2,1,0:T(8,128)}, /*index=5*/bf16[128,8,128]{2,1,0:T(8,128)(2,1)}) custom-call(bf16[1024,3072]{1,0:T(8,128)(2,1)} %bitcast.6, bf16[64,3072]{1,0:T(8,128)(2,1)} %bitcast.7, bf16[64,3072]{1,0:T(8,128)(2,1)} %bitcast.8, ...), custom_call_target="tpu_custom_call" | custom-call | tf_op jit(solution)/shard_map/pallas_call | solution.py:917
  89.4 1.9 %shard_map.110 = (f32[24,64]{1,0:T(8,128)}, f32[24,64]{1,0:T(8,128)}, f32[64,64]{1,0:T(8,128)}, f32[64,8,128]{2,1,0:T(8,128)}, f32[4,8,128]{2,1,0:T(8,128)}, /*index=5*/bf16[128,8,128]{2,1,0:T(8,128)(2,1)}) custom-call(f32[24,64]{1,0:T(8,128)} %get-tuple-element.18.refs_0_, f32[24,64]{1,0:T(8,128)} %get-tuple-element.19.refs_1_, ...), custom_call_target="tpu_custom_call" | custom-call | tf_op jit(solution)/shard_map/pallas_call | solution.py:934

commit v3 on v2

--- a/solution.py
+++ b/solution.py
@@ -39,6 +39,12 @@
         return carry
 
     lax.fori_loop(0, count, step, 0)
+
+
+def when(test):
+    if isinstance(test, bool):
+        return (lambda body: body()) if test else (lambda body: None)
+    return pl.when(test)
 
 
 def split_2(value):
@@ -80,7 +86,7 @@
     recv_pick,
     recv_pick_t,
     xp,
-    xp_low,
+    xp_t,
     ex_src,
     ex_dst,
     low_in,
@@ -142,7 +148,7 @@
     lats = discw.shape[1]
     portion = bins // n_dev
     n_group = n_row // 2
-    n_pair = n_group // 2
+    few = min(4, n_group)
     width = 2 * LANES
     per_dev = genes // n_dev
     span = genes // n_group
@@ -171,6 +177,9 @@
             ]
         )
     ]
+
+    def bins_of(i, size=LANES):
+        return pl.ds(i * size if isinstance(i, int) else pl.multiple_of(i * size, size), size)
 
     def swap(value):
         return pltpu.roll(value, lats, value.ndim - 1)
@@ -276,9 +285,6 @@
         each(LANES // SIDE + 2, down)
         each(rows, along)
 
-    def bins_of(i, size=LANES):
-        return pl.ds(pl.multiple_of(i * size, size), size)
-
     def put(turn, i, value):
         pads[turn % 2, i + RADIUS, SIDE : SIDE + LANES, :] = value
         low = value.astype(BF16)
@@ -293,11 +299,11 @@
         else:
             packed = jnp.where(first, swap(front), rear).astype(BF16)
 
-        @pl.when(i < RADIUS)
+        @when(i < RADIUS)
         def _():
             pack_src[PACKED[turn], 0, i] = packed
 
-        @pl.when(i >= rows - RADIUS)
+        @when(i >= rows - RADIUS)
         def _():
             pack_src[PACKED[turn], 1, i - (rows - RADIUS)] = packed
 
@@ -432,31 +438,24 @@
         return carry
 
     lax.fori_loop(1, n_col, greet_meet, 0)
-    def project(i):
-        for k in range(rows // CHUNKS):
-            at = i * (rows // CHUNKS) + k
-            pltpu.make_async_copy(
-                feat_hbm.at[bins_of(at)], x.at[bins_of(at)], feat_sem.at[at]
-            ).wait()
-        acc = dot(x[bins_of(i, chunk), :], wcat[...], 1, 1)
-        xp[bins_of(i, chunk), :] = acc
-        xp_low[bins_of(i, chunk), :] = acc.astype(BF16)
-
-    each(CHUNKS, project)
-
-    def pick_out(i):
-        value = dot(send_pick[bins_of(i, chunk), :], xp_low[...])
-        ex_src[0, pl.ds(i * (n_dev // CHUNKS), n_dev // CHUNKS)] = value.astype(BF16).reshape(
-            n_dev // CHUNKS, portion, LANES
-        )
-
-    each(CHUNKS, pick_out)
+    for k in range(rows):
+        pltpu.make_async_copy(feat_hbm.at[bins_of(k)], x.at[bins_of(k)], feat_sem.at[k]).wait()
+    flat = dot(wcat[...], x[...], 1, 1)
+    xp_t[...] = flat
+    picked = dot(flat.astype(BF16), send_pick[...], 1, 1)
+    each_dev = LANES // portion
+    for i in range(rows):
+        block = picked[:, i * LANES : (i + 1) * LANES].T.astype(BF16)
+        ex_src[0, i * each_dev : (i + 1) * each_dev] = block.reshape(each_dev, portion, LANES)
 
     pl.semaphore_wait(meet_sem, n_col - 1)
 
     ex_start(0)
 
-    each(rows, lambda i: put(0, i, swap(xp_low[bins_of(i), :].astype(F32))))
+    for i in range(rows):
+        block = xp_t[:, i * LANES : (i + 1) * LANES].T
+        xp[bins_of(i), :] = block
+        put(0, i, swap(block.astype(BF16).astype(F32)))
     halo_start(0)
     build_recv()
     def elu(value):
@@ -525,19 +524,19 @@
 
     def rs1_run(which, product):
         def body(k):
-            pair = lax.rem(my_group // 2 + 1 + k, n_pair)
-            where = bins_of(pair, 2 * span)
+            part = lax.rem(my_group // few + 1 + k, n_group // few)
+            where = bins_of(part, few * span)
             value = product(where).astype(BF16)
-            for j in range(4):
+            for j in range(2 * few):
                 at = (j // 2) * span + (j % 2) * LANES
-                rs1_src[which, 4 * pair + j] = value[:, at : at + width]
-            for j in range(4):
-
-                @pl.when(4 * pair + j != r)
+                rs1_src[which, 2 * few * part + j] = value[:, at : at + width]
+            for j in range(2 * few):
+
+                @pl.when(2 * few * part + j != r)
                 def _():
-                    rs1_copy(which, 4 * pair + j).start()
-
-        each(n_pair, body)
+                    rs1_copy(which, 2 * few * part + j).start()
+
+        each(n_group // few, body)
 
     def rs1_finish(which):
         drain(rs1_dst.at[which], n_row, r1s_sem.at[which], r1r_sem.at[which])
@@ -646,7 +645,8 @@
         for j in range(step):
             put(3, i * step + j, spread_grad[j * LANES : (j + 1) * LANES, :])
 
-    each(CHUNKS, contrast)
+    for i in range(CHUNKS):
+        contrast(i)
     halo_start(3)
 
     def disc_step(i, total):
@@ -857,7 +857,7 @@
         vmem((bins, bins), BF16),
         vmem((bins, bins), BF16),
         vmem((bins, LANES), F32),
-        vmem((bins, LANES), BF16),
+        vmem((LANES, bins), F32),
         vmem((2, n_dev, portion, LANES), BF16),
         vmem((2, n_dev, portion, LANES), BF16),
         vmem((bins, LANES), BF16),

time: 91.5 us -> 91.4 us (level)
  no operation moved by 1% of the time
where the time goes in v3:
time: 91.4 us; the launch traced here: 91.2 us
  Pallas kernels  90.6 us (99%)
    pallas_call x1, Pallas kernels, per_device(): pl.pallas_call(functools.partial(kernel, n_row, n_col), out_shape=out_sha...  88.7 us
    pallas_call x1, Pallas kernels, per_device(): pl.pallas_call(hand_on, out_shape=out_shape, in_specs=anywhere, out_specs...  1.91 us

profile of v3, /device:TPU:1, one launch (start us, length us, event | category | flops | bytes accessed | tf_op | source)
XLA Modules:
  0.0 91.2 jit_solution(834497727568246600)
XLA Ops:
  0.6 88.7 %shard_map.109 = (f32[24,64]{1,0:T(8,128)}, f32[24,64]{1,0:T(8,128)}, f32[64,64]{1,0:T(8,128)}, f32[64,8,128]{2,1,0:T(8,128)}, f32[4,8,128]{2,1,0:T(8,128)}, /*index=5*/bf16[128,8,128]{2,1,0:T(8,128)(2,1)}) custom-call(bf16[1024,3072]{1,0:T(8,128)(2,1)} %bitcast.6, bf16[64,3072]{1,0:T(8,128)(2,1)} %bitcast.7, bf16[64,3072]{1,0:T(8,128)(2,1)} %bitcast.8, ...), custom_call_target="tpu_custom_call" | custom-call | tf_op jit(solution)/shard_map/pallas_call | solution.py:917
  89.3 1.9 %shard_map.110 = (f32[24,64]{1,0:T(8,128)}, f32[24,64]{1,0:T(8,128)}, f32[64,64]{1,0:T(8,128)}, f32[64,8,128]{2,1,0:T(8,128)}, f32[4,8,128]{2,1,0:T(8,128)}, /*index=5*/bf16[128,8,128]{2,1,0:T(8,128)(2,1)}) custom-call(f32[24,64]{1,0:T(8,128)} %get-tuple-element.18.refs_0_, f32[24,64]{1,0:T(8,128)} %get-tuple-element.19.refs_1_, ...), custom_call_target="tpu_custom_call" | custom-call | tf_op jit(solution)/shard_map/pallas_call | solution.py:934

commit v4 on v3

--- a/solution.py
+++ b/solution.py
@@ -87,6 +87,10 @@
     recv_pick_t,
     xp,
     xp_t,
+    row_src,
+    row_dst,
+    col_src,
+    col_dst,
     ex_src,
     ex_dst,
     low_in,
@@ -362,7 +366,7 @@
             line = orders[1, pl.ds(a, 1), :].astype(F32)
             column = jnp.broadcast_to(line, (LANES, LANES)).T
             for t in range(rows):
-                index = (lane + t * LANES).astype(F32)
+                index = recv_index(lane + t * LANES)
                 recv_pick[
                     pl.ds(pl.multiple_of(a * LANES, LANES), LANES), t * LANES : (t + 1) * LANES
                 ] = jnp.where(column == index, 1.0, 0.0).astype(BF16)
@@ -382,13 +386,46 @@
 
         lax.fori_loop(0, rows, body, 0)
 
-    def ex_copy(which, k):
+    def regroup(values):
+        m = values.shape[0] // 2
+        n = values.shape[1] // portion
+        low, high = values[:m], values[m:]
+        parts = []
+        for value in (jnp.where(first, low, swap(high)), jnp.where(first, swap(low), high)):
+            for k in range(n):
+                block = value[:, k * portion : (k + 1) * portion, :]
+                parts.append(block.reshape(m * portion, LANES))
+        return parts
+
+    def row_copy(k):
+        other = lax.rem(r + k, n_row)
+        return pltpu.make_async_remote_copy(
+            src_ref=row_src.at[other],
+            dst_ref=row_dst.at[r],
+            send_sem=as_sem.at[0],
+            recv_sem=ar_sem.at[0],
+            device_id=(other, c),
+            device_id_type=MESH,
+        )
+
+    def col_copy(k):
+        other = lax.rem(c + k, n_col)
+        return pltpu.make_async_remote_copy(
+            src_ref=col_src.at[other],
+            dst_ref=col_dst.at[c],
+            send_sem=as_sem.at[1],
+            recv_sem=ar_sem.at[1],
+            device_id=(r, other),
+            device_id_type=MESH,
+        )
+
+    def ex_copy(k):
         other = lax.rem(me + k, n_dev)
         return pltpu.make_async_remote_copy(
-            src_ref=ex_src.at[which, other],
-            dst_ref=ex_dst.at[which, me],
-            send_sem=as_sem.at[which],
-            recv_sem=ar_sem.at[which],
+            src_ref=ex_src.at[other],
+            dst_ref=ex_dst.at[me],
+            send_sem=as_sem.at[2],
+            recv_sem=ar_sem.at[2],
             device_id=(other // n_col, lax.rem(other, n_col)),
             device_id_type=MESH,
         )
@@ -405,13 +442,14 @@
         pltpu.make_async_copy(most, most, recv_sem).wait()
         pltpu.make_async_copy(most, most, send_sem).wait()
 
-    def ex_start(which):
-        peers(n_dev, functools.partial(ex_copy, which))
-        ex_dst[which, me] = ex_src[which, me]
-
-    def ex_wait(which):
-        drain(ex_dst.at[which], n_dev, as_sem.at[which], ar_sem.at[which])
-        return ex_dst[which].reshape(bins, LANES)
+    def recv_index(position):
+        slot = lax.rem(position, portion)
+        rest = position // portion
+        low_row = lax.rem(rest, n_row // 2)
+        rest = rest // (n_row // 2)
+        col = lax.rem(rest, n_col)
+        row = (rest // n_col) * (n_row // 2) + low_row
+        return (((row * n_col) + col) * portion + slot).astype(F32)
 
     loads[0].wait()
     loads[1].wait()
@@ -443,14 +481,15 @@
     flat = dot(wcat[...], x[...], 1, 1)
     xp_t[...] = flat
     picked = dot(flat.astype(BF16), send_pick[...], 1, 1)
-    each_dev = LANES // portion
-    for i in range(rows):
-        block = picked[:, i * LANES : (i + 1) * LANES].T.astype(BF16)
-        ex_src[0, i * each_dev : (i + 1) * each_dev] = block.reshape(each_dev, portion, LANES)
+    turned = jnp.concatenate(
+        [picked[:, i * LANES : (i + 1) * LANES].T for i in range(rows)], axis=0
+    ).reshape(n_row, 2, n_col // 2 * portion, LANES)
+    row_src[...] = jnp.where(first, swap(turned[:, 0]), turned[:, 1]).astype(BF16)
 
     pl.semaphore_wait(meet_sem, n_col - 1)
 
-    ex_start(0)
+    peers(n_row, row_copy)
+    row_dst[r] = row_src[r]
 
     for i in range(rows):
         block = xp_t[:, i * LANES : (i + 1) * LANES].T
@@ -458,6 +497,12 @@
         put(0, i, swap(block.astype(BF16).astype(F32)))
     halo_start(0)
     build_recv()
+    drain(row_dst, n_row, as_sem.at[0], ar_sem.at[0])
+    for k, value in enumerate(regroup(row_dst[...].astype(F32))):
+        col_src[k] = value.astype(BF16)
+    peers(n_col, col_copy)
+    col_dst[c] = col_src[c]
+
     def elu(value):
         return jnp.where(value > 0, value, jnp.exp(jnp.minimum(value, 0.0)) - 1.0)
 
@@ -468,11 +513,14 @@
     halo_take(0)
     stencil(0, first_latent)
 
-    arrived = ex_wait(0)
-    low_in[...] = arrived
+    drain(col_dst, n_col, as_sem.at[1], ar_sem.at[1])
+    low_in[...] = col_dst[...].reshape(bins // 2, LANES)
 
     def pick_in(i):
-        value = dot(recv_pick[bins_of(i, chunk), :], low_in[...])
+        here = bins_of(i, chunk)
+        value = swap(dot(recv_pick[here, : bins // 2], low_in[...])) + dot(
+            recv_pick[here, bins // 2 :], low_in[...]
+        )
         for k in range(rows // CHUNKS):
             at = i * (rows // CHUNKS) + k
             put(1, at, jnp.where(first, emb[at], value[k * LANES : (k + 1) * LANES, :]))
@@ -574,17 +622,6 @@
         mine = by_gene[pl.ds(pl.multiple_of(begin + c * per_dev, 8), per_dev), :]
         norm_src[which] = jnp.broadcast_to(jnp.sum(own_genes * own_genes), (8, LANES))
         return mine
-
-    square = dot(lt[0:lats, :], s_low[...])
-    square_high = square.astype(BF16).astype(F32)
-    square2 = jnp.where(first, square_high, square - square_high).astype(BF16)
-    loads[4].wait()
-    loads[5].wait()
-    rs1_run(
-        0,
-        lambda where: slope_scale
-        * (dot(square2, wtwice[:, where]) - dot(lt[0:lats, :], x[:, where])),
-    )
 
     loads[6].wait()
     wide = jnp.concatenate([discw[...], jnp.zeros_like(discw)], axis=1)
@@ -684,9 +721,6 @@
             at = k * (lats // 2)
             log_out[k, i : i + 1, :] = flipped[at : at + 1, :]
     outs[4].start()
-    rs1_finish(0)
-    rs2_start(0)
-
     halo_take(3)
 
     def to_latent_grad(i, value):
@@ -713,7 +747,16 @@
 
     disc_b[r] = disc_bsrc[...]
     peers(n_row, disc_2)
-    dec_sum[...] = rs2_finish(0)
+    square = dot(lt[0:lats, :], s_low[...])
+    square_high = square.astype(BF16).astype(F32)
+    square2 = jnp.where(first, square_high, square - square_high).astype(BF16)
+    loads[4].wait()
+    loads[5].wait()
+    rs1_run(
+        0,
+        lambda where: slope_scale
+        * (dot(square2, wtwice[:, where]) - dot(lt[0:lats, :], x[:, where])),
+    )
 
     halo_take(4)
 
@@ -724,12 +767,13 @@
 
     def pick_back(i):
         value = dot(recv_pick_t[bins_of(i, chunk), :], pg_low[...])
-        ex_src[1, pl.ds(i * (n_dev // CHUNKS), n_dev // CHUNKS)] = value.astype(BF16).reshape(
+        ex_src[pl.ds(i * (n_dev // CHUNKS), n_dev // CHUNKS)] = value.astype(BF16).reshape(
             n_dev // CHUNKS, portion, LANES
         )
 
     each(CHUNKS, pick_back)
-    ex_start(1)
+    peers(n_dev, ex_copy)
+    ex_dst[me] = ex_src[me]
     for i in range(rows):
         here = slice(i * LANES, (i + 1) * LANES)
         flipped = pg_low[here, :].astype(F32).T
@@ -738,6 +782,8 @@
     pg_out[...] = stage[...].astype(BF16)
     outs[5].start()
 
+    rs1_finish(0)
+    rs2_start(0)
     drain(disc_b, n_row, ds_sem.at[1], dr_sem.at[1])
     disc_full[c] = jnp.sum(disc_b[...], axis=0)
 
@@ -758,7 +804,8 @@
         halo_finish(turn)
 
     lt[0:lats, :] = own[...]
-    home = ex_wait(1)
+    drain(ex_dst, n_dev, as_sem.at[2], ar_sem.at[2])
+    home = ex_dst[...].reshape(bins, LANES)
     flipped = jnp.concatenate(
         [home[i * LANES : (i + 1) * LANES, :].astype(F32).T[lats:, :] for i in range(rows)], axis=1
     ).astype(BF16)
@@ -776,6 +823,7 @@
     disc_out[...] = disc_grad * lax.rsqrt(disc_mean + 1e-06)
     outs[2].start()
 
+    dec_sum[...] = rs2_finish(0)
     rs1_finish(1)
     rs2_start(1)
     enc_sum = rs2_finish(1)
@@ -858,9 +906,13 @@
         vmem((bins, bins), BF16),
         vmem((bins, LANES), F32),
         vmem((LANES, bins), F32),
-        vmem((2, n_dev, portion, LANES), BF16),
-        vmem((2, n_dev, portion, LANES), BF16),
-        vmem((bins, LANES), BF16),
+        vmem((n_row, n_col // 2 * portion, LANES), BF16),
+        vmem((n_row, n_col // 2 * portion, LANES), BF16),
+        vmem((n_col, n_row // 2 * portion, LANES), BF16),
+        vmem((n_col, n_row // 2 * portion, LANES), BF16),
+        vmem((n_dev, portion, LANES), BF16),
+        vmem((n_dev, portion, LANES), BF16),
+        vmem((bins // 2, LANES), BF16),
         vmem((2, tile_rows + 2 * RADIUS, LANES + 2 * SIDE, LANES), F32),
         vmem((tile_rows, LANES + 2 * SIDE, LANES), F32),
         vmem((ROUNDS,) + field, BF16),
@@ -900,8 +952,8 @@
         dma((tile_rows,)),
         dma((ROUNDS, 8)),
         dma((ROUNDS, 8)),
-        dma((2,)),
-        dma((2,)),
+        dma((3,)),
+        dma((3,)),
         dma((2,)),
         dma((2,)),
         dma((2,)),

time: 91.4 us -> 92.1 us (level)
  no operation moved by 1% of the time
where the time goes in v4:
time: 92.1 us; the launch traced here: 92 us
  Pallas kernels  91.3 us (99%)
    pallas_call x1, Pallas kernels, per_device(): pl.pallas_call(functools.partial(kernel, n_row, n_col), out_shape=out_sha...  89.4 us
    pallas_call x1, Pallas kernels, per_device(): pl.pallas_call(hand_on, out_shape=out_shape, in_specs=anywhere, out_specs...  1.91 us

profile of v4, /device:TPU:1, one launch (start us, length us, event | category | flops | bytes accessed | tf_op | source)
XLA Modules:
  0.0 92.0 jit_solution(6305513262742661934)
XLA Ops:
  0.6 89.4 %shard_map.109 = (f32[24,64]{1,0:T(8,128)}, f32[24,64]{1,0:T(8,128)}, f32[64,64]{1,0:T(8,128)}, f32[64,8,128]{2,1,0:T(8,128)}, f32[4,8,128]{2,1,0:T(8,128)}, /*index=5*/bf16[128,8,128]{2,1,0:T(8,128)(2,1)}) custom-call(bf16[1024,3072]{1,0:T(8,128)(2,1)} %bitcast.6, bf16[64,3072]{1,0:T(8,128)(2,1)} %bitcast.7, bf16[64,3072]{1,0:T(8,128)(2,1)} %bitcast.8, ...), custom_call_target="tpu_custom_call" | custom-call | tf_op jit(solution)/shard_map/pallas_call | solution.py:969
  90.1 1.9 %shard_map.110 = (f32[24,64]{1,0:T(8,128)}, f32[24,64]{1,0:T(8,128)}, f32[64,64]{1,0:T(8,128)}, f32[64,8,128]{2,1,0:T(8,128)}, f32[4,8,128]{2,1,0:T(8,128)}, /*index=5*/bf16[128,8,128]{2,1,0:T(8,128)(2,1)}) custom-call(f32[24,64]{1,0:T(8,128)} %get-tuple-element.18.refs_0_, f32[24,64]{1,0:T(8,128)} %get-tuple-element.19.refs_1_, ...), custom_call_target="tpu_custom_call" | custom-call | tf_op jit(solution)/shard_map/pallas_call | solution.py:986

commit v5 on v4

--- a/solution.py
+++ b/solution.py
@@ -11,7 +11,6 @@
 RADIUS = 3
 RECON_WEIGHT = 10.0
 LANES = 128
-EDGE = 16
 SIDE = 8
 MESH = pl.DeviceIdType.MESH
 F32 = jnp.float32
@@ -102,6 +101,8 @@
     h_corner,
     pack_src,
     h_pack,
+    edge,
+    edge_src,
     lat,
     emb,
     spread,
@@ -115,6 +116,9 @@
     pg_low,
     lt,
     own,
+    rs0_keep,
+    rs0_src,
+    rs0_dst,
     rs1_src,
     rs1_dst,
     rs2_src,
@@ -135,6 +139,8 @@
     hr_sem,
     as_sem,
     ar_sem,
+    r0s_sem,
+    r0r_sem,
     r1s_sem,
     r1r_sem,
     r2s_sem,
@@ -153,7 +159,6 @@
     portion = bins // n_dev
     n_group = n_row // 2
     few = min(4, n_group)
-    width = 2 * LANES
     per_dev = genes // n_dev
     span = genes // n_group
     part = lats // n_col
@@ -197,13 +202,17 @@
 
     def halo_copy(turn, way):
         dr, dc = DIRECTIONS[way]
-        row_part = pl.ds(0, RADIUS) if dr < 0 else pl.ds(rows - RADIUS, RADIUS) if dr else pl.ds(0, rows)
-        col_part = pl.ds(0, EDGE) if dc < 0 else pl.ds(LANES - EDGE, EDGE) if dc else pl.ds(0, LANES)
         if way < 2 and turn in PACKED:
             source = pack_src.at[PACKED[turn], way]
             target = h_pack.at[PACKED[turn], OPPOSITE[way]]
+        elif way < 2:
+            source = hsrc.at[turn, pl.ds(0 if dr < 0 else rows - RADIUS, RADIUS)]
+            target = halo_buffer(turn, OPPOSITE[way])
         else:
-            source = hsrc.at[turn, row_part, col_part]
+            half = rows * SIDE // 2
+            source = edge_src.at[turn, 0 if dc < 0 else 1]
+            if dr:
+                source = source.at[pl.ds(0 if dr < 0 else half, half)]
             target = halo_buffer(turn, OPPOSITE[way])
         return pltpu.make_async_remote_copy(
             src_ref=source,
@@ -228,6 +237,7 @@
         return functools.reduce(jnp.logical_and, tests)
 
     def halo_start(turn):
+        edge_src[turn] = edge[...].astype(BF16)
         for way in range(8):
 
             @pl.when(present(way))
@@ -252,11 +262,13 @@
                 pad[part, SIDE + LANES // 2 : SIDE + LANES, :] = halves[1]
             else:
                 pad[part, SIDE : SIDE + LANES, :] = h_row[turn, way].astype(F32)
-            pad[part, left, :] = h_corner[turn, 2 * way].astype(F32)[:, EDGE - SIDE :, :]
-            pad[part, right, :] = h_corner[turn, 2 * way + 1].astype(F32)[:, :SIDE, :]
+            lines = slice(rows // 2 - RADIUS, rows // 2) if way == 0 else slice(0, RADIUS)
+            for k, place in ((0, left), (1, right)):
+                corner = h_corner[turn, 2 * way + k].astype(F32).reshape(rows // 2, SIDE, LANES)
+                pad[part, place, :] = corner[lines]
         own_rows = slice(RADIUS, RADIUS + rows)
-        pad[own_rows, left, :] = h_col[turn, 0].astype(F32)[:, EDGE - SIDE :, :]
-        pad[own_rows, right, :] = h_col[turn, 1].astype(F32)[:, :SIDE, :]
+        for k, place in ((0, left), (1, right)):
+            pad[own_rows, place, :] = h_col[turn, k].astype(F32).reshape(rows, SIDE, LANES)
 
     def halo_finish(turn):
         for way in range(8):
@@ -291,12 +303,11 @@
 
     def put(turn, i, value):
         pads[turn % 2, i + RADIUS, SIDE : SIDE + LANES, :] = value
-        low = value.astype(BF16)
+        edge[0, bins_of(i, SIDE), :] = value[0:SIDE, :]
+        edge[1, bins_of(i, SIDE), :] = value[LANES - SIDE :, :]
         if turn not in PACKED:
-            hsrc[turn, i] = low
+            hsrc[turn, i] = value.astype(BF16)
             return
-        hsrc[turn, i, 0:EDGE, :] = low[0:EDGE, :]
-        hsrc[turn, i, LANES - EDGE :, :] = low[LANES - EDGE :, :]
         front, rear = value[: LANES // 2, :], value[LANES // 2 :, :]
         if turn == 0:
             packed = jnp.where(first, front, swap(rear)).astype(BF16)
@@ -560,37 +571,70 @@
         dot(s_low[...], gram2[...]) - jnp.where(first, xp[...], 0.0)
     )
 
-    def rs1_copy(which, target):
+    core = lax.rem(r, 2)
+    n_part = n_group // few
+
+    def part_at(k):
+        return lax.rem(my_group // few + 1 + k, n_part)
+
+    def rs0_copy(which, k):
+        here = pl.ds(part_at(k) * few, few)
         return pltpu.make_async_remote_copy(
-            src_ref=rs1_src.at[which, target],
-            dst_ref=rs1_dst.at[which, r],
-            send_sem=r1s_sem.at[which],
-            recv_sem=r1r_sem.at[which],
-            device_id=(target, c),
+            src_ref=rs0_src.at[which, here],
+            dst_ref=rs0_dst.at[which, here],
+            send_sem=r0s_sem.at[which, k],
+            recv_sem=r0r_sem.at[which, k],
+            device_id=(r + 1 - 2 * core, c),
             device_id_type=MESH,
         )
 
-    def rs1_run(which, product):
+    def rs0_run(which, product):
         def body(k):
-            part = lax.rem(my_group // few + 1 + k, n_group // few)
-            where = bins_of(part, few * span)
-            value = product(where).astype(BF16)
-            for j in range(2 * few):
-                at = (j // 2) * span + (j % 2) * LANES
-                rs1_src[which, 2 * few * part + j] = value[:, at : at + width]
-            for j in range(2 * few):
-
-                @pl.when(2 * few * part + j != r)
+            part = part_at(k)
+            value = product(bins_of(part, few * span))
+            for j in range(few):
+                at = j * span
+                middle = value[:, at + LANES : at + 2 * LANES]
+                top, bottom = middle[: lats // 2, :], middle[lats // 2 :, :]
+                lower = jnp.concatenate(
+                    [value[:, at : at + LANES], jnp.where(first, top, swap(bottom))], axis=0
+                )
+                upper = jnp.concatenate(
+                    [value[:, at + 2 * LANES : at + span], jnp.where(first, swap(top), bottom)],
+                    axis=0,
+                )
+                rs0_keep[which, part * few + j] = jnp.where(core == 0, lower, upper)
+                rs0_src[which, part * few + j] = jnp.where(core == 0, upper, lower).astype(BF16)
+            rs0_copy(which, k).start()
+
+        each(n_part, body)
+
+    def rs1_start(which):
+        def body(k):
+            rs0_copy(which, k).wait()
+            for j in range(few):
+                group = part_at(k) * few + j
+                total = rs0_keep[which, group] + rs0_dst[which, group].astype(F32)
+                rs1_src[which, group] = total.astype(BF16)
+
+                @pl.when(group != my_group)
                 def _():
-                    rs1_copy(which, 2 * few * part + j).start()
-
-        each(n_group // few, body)
+                    pltpu.make_async_remote_copy(
+                        src_ref=rs1_src.at[which, group],
+                        dst_ref=rs1_dst.at[which, my_group],
+                        send_sem=r1s_sem.at[which],
+                        recv_sem=r1r_sem.at[which],
+                        device_id=(2 * group + core, c),
+                        device_id_type=MESH,
+                    ).start()
+
+        each(n_part, body)
 
     def rs1_finish(which):
-        drain(rs1_dst.at[which], n_row, r1s_sem.at[which], r1r_sem.at[which])
-        rs1_dst[which, r] = rs1_src[which, r]
+        drain(rs1_dst.at[which], n_group, r1s_sem.at[which], r1r_sem.at[which])
+        rs1_dst[which, my_group] = rs1_src[which, my_group]
         total = rs1_dst[which, 0].astype(F32)
-        for k in range(1, n_row):
+        for k in range(1, n_group):
             total += rs1_dst[which, k].astype(F32)
         rs2_src[which] = total.astype(BF16)
 
@@ -614,14 +658,12 @@
         total = rs2_dst[which, 0].astype(F32)
         for k in range(1, n_col):
             total += rs2_dst[which, k].astype(F32)
-        begin = lax.rem(r, 2) * (width - span // 2)
-        gene = lax.broadcasted_iota(jnp.int32, (1, width), 1) - begin
-        own_genes = jnp.where((gene >= 0) & (gene < span // 2), total, 0.0)
-        for k in range(width // LANES):
-            by_gene[k * LANES : (k + 1) * LANES, :] = total[:, k * LANES : (k + 1) * LANES].T
-        mine = by_gene[pl.ds(pl.multiple_of(begin + c * per_dev, 8), per_dev), :]
-        norm_src[which] = jnp.broadcast_to(jnp.sum(own_genes * own_genes), (8, LANES))
-        return mine
+        norm_src[which] = jnp.broadcast_to(jnp.sum(total * total), (8, LANES))
+        pairs = total[lats:, :]
+        pairs = jnp.concatenate([pairs, swap(pairs)], axis=0).T
+        by_gene[pl.ds(pl.multiple_of(core * lats, lats), LANES), :] = total[:lats, :].T
+        by_gene[pl.ds(pl.multiple_of((1 - core) * LANES, LANES), lats), :] = pairs[:lats, :]
+        return by_gene[pl.ds(pl.multiple_of(c * per_dev, 8), per_dev), :]
 
     loads[6].wait()
     wide = jnp.concatenate([discw[...], jnp.zeros_like(discw)], axis=1)
@@ -721,6 +763,17 @@
             at = k * (lats // 2)
             log_out[k, i : i + 1, :] = flipped[at : at + 1, :]
     outs[4].start()
+    square = dot(lt[0:lats, :], s_low[...])
+    square_high = square.astype(BF16).astype(F32)
+    square2 = jnp.where(first, square_high, square - square_high).astype(BF16)
+    loads[4].wait()
+    loads[5].wait()
+    rs0_run(
+        0,
+        lambda where: slope_scale
+        * (dot(square2, wtwice[:, where]) - dot(lt[0:lats, :], x[:, where])),
+    )
+
     halo_take(3)
 
     def to_latent_grad(i, value):
@@ -747,17 +800,7 @@
 
     disc_b[r] = disc_bsrc[...]
     peers(n_row, disc_2)
-    square = dot(lt[0:lats, :], s_low[...])
-    square_high = square.astype(BF16).astype(F32)
-    square2 = jnp.where(first, square_high, square - square_high).astype(BF16)
-    loads[4].wait()
-    loads[5].wait()
-    rs1_run(
-        0,
-        lambda where: slope_scale
-        * (dot(square2, wtwice[:, where]) - dot(lt[0:lats, :], x[:, where])),
-    )
-
+    rs1_start(0)
     halo_take(4)
 
     def to_proj_grad(i, value):
@@ -783,7 +826,6 @@
     outs[5].start()
 
     rs1_finish(0)
-    rs2_start(0)
     drain(disc_b, n_row, ds_sem.at[1], dr_sem.at[1])
     disc_full[c] = jnp.sum(disc_b[...], axis=0)
 
@@ -805,6 +847,7 @@
 
     lt[0:lats, :] = own[...]
     drain(ex_dst, n_dev, as_sem.at[2], ar_sem.at[2])
+    rs2_start(0)
     home = ex_dst[...].reshape(bins, LANES)
     flipped = jnp.concatenate(
         [home[i * LANES : (i + 1) * LANES, :].astype(F32).T[lats:, :] for i in range(rows)], axis=1
@@ -815,7 +858,8 @@
         value = dot(lt[...], x[:, where])
         return value[:lats, :] + value[lats:, :]
 
-    rs1_run(1, encoder_part)
+    rs0_run(1, encoder_part)
+    rs1_start(1)
 
     drain(disc_full, n_col, ds_sem.at[2], dr_sem.at[2])
     disc_grad = disc_full[...].reshape(lats, LANES)[:, :lats]
@@ -878,6 +922,7 @@
     per_dev = genes // n_dev
     span = genes // n_group
     part = lats // n_col
+    packed = lats + lats // 2
     portion = bins // n_dev
     field = (tile_rows, LANES, LANES)
     dma = pltpu.SemaphoreType.DMA
@@ -917,10 +962,12 @@
         vmem((tile_rows, LANES + 2 * SIDE, LANES), F32),
         vmem((ROUNDS,) + field, BF16),
         vmem((ROUNDS, 2, RADIUS, LANES, LANES), BF16),
-        vmem((ROUNDS, 2, tile_rows, EDGE, LANES), BF16),
-        vmem((ROUNDS, 4, RADIUS, EDGE, LANES), BF16),
+        vmem((ROUNDS, 2, tile_rows * SIDE, LANES), BF16),
+        vmem((ROUNDS, 4, tile_rows * SIDE // 2, LANES), BF16),
         vmem((len(PACKED), 2, RADIUS, LANES // 2, LANES), BF16),
         vmem((len(PACKED), 2, RADIUS, LANES // 2, LANES), BF16),
+        vmem((2, tile_rows * SIDE, LANES), F32),
+        vmem((ROUNDS, 2, tile_rows * SIDE, LANES), BF16),
         vmem(field, F32),
         vmem(field, F32),
         vmem(field, F32),
@@ -934,10 +981,13 @@
         vmem((bins, LANES), BF16),
         vmem((LANES, bins), BF16),
         vmem((lats, bins), BF16),
-        vmem((2, n_row, lats, 2 * LANES), BF16),
-        vmem((2, n_row, lats, 2 * LANES), BF16),
-        vmem((2, lats, 2 * LANES), BF16),
-        vmem((2, n_col, lats, 2 * LANES), BF16),
+        vmem((2, n_group, packed, LANES), F32),
+        vmem((2, n_group, packed, LANES), BF16),
+        vmem((2, n_group, packed, LANES), BF16),
+        vmem((2, n_group, packed, LANES), BF16),
+        vmem((2, n_group, packed, LANES), BF16),
+        vmem((2, packed, LANES), BF16),
+        vmem((2, n_col, packed, LANES), BF16),
         vmem((lats, LANES), F32),
         vmem((n_col, part, LANES), F32),
         vmem((part, LANES), F32),
@@ -945,7 +995,7 @@
         vmem((n_col, part, LANES), F32),
         vmem((2, 8, LANES), F32),
         vmem((n_row, 2, 8, LANES), F32),
-        vmem((2 * LANES, lats), F32),
+        vmem((span // 2, lats), F32),
         vmem((LANES, tile_rows, LANES), F32),
         vmem((per_dev, lats), F32),
         dma((7,)),
@@ -954,6 +1004,8 @@
         dma((ROUNDS, 8)),
         dma((3,)),
         dma((3,)),
+        dma((2, 2)),
+        dma((2, 2)),
         dma((2,)),
         dma((2,)),
         dma((2,)),

time: 92.1 us -> 83.7 us (0.909)
  Pallas kernels: 91.3 us -> 82.8 us
    pallas_call x1, Pallas kernels: 89.4 us -> 80.9 us  [per_device(): pl.pallas_call(functools.partial(kernel, n_row, n_col), out_shape=out_sha...]
where the time goes in v5:
time: 83.7 us; the launch traced here: 83.5 us
  Pallas kernels  82.8 us (99%)
    pallas_call x1, Pallas kernels, per_device(): pl.pallas_call(functools.partial(kernel, n_row, n_col), out_shape=out_sha...  80.9 us
    pallas_call x1, Pallas kernels, per_device(): pl.pallas_call(hand_on, out_shape=out_shape, in_specs=anywhere, out_specs...  1.91 us

profile of v5, /device:TPU:1, one launch (start us, length us, event | category | flops | bytes accessed | tf_op | source)
XLA Modules:
  0.0 83.5 jit_solution(1106076085433576688)
XLA Ops:
  0.6 80.9 %shard_map.109 = (f32[24,64]{1,0:T(8,128)}, f32[24,64]{1,0:T(8,128)}, f32[64,64]{1,0:T(8,128)}, f32[64,8,128]{2,1,0:T(8,128)}, f32[4,8,128]{2,1,0:T(8,128)}, /*index=5*/bf16[128,8,128]{2,1,0:T(8,128)(2,1)}) custom-call(bf16[1024,3072]{1,0:T(8,128)(2,1)} %bitcast.6, bf16[64,3072]{1,0:T(8,128)(2,1)} %bitcast.7, bf16[64,3072]{1,0:T(8,128)(2,1)} %bitcast.8, ...), custom_call_target="tpu_custom_call" | custom-call | tf_op jit(solution)/shard_map/pallas_call | solution.py:1021
  81.6 1.9 %shard_map.110 = (f32[24,64]{1,0:T(8,128)}, f32[24,64]{1,0:T(8,128)}, f32[64,64]{1,0:T(8,128)}, f32[64,8,128]{2,1,0:T(8,128)}, f32[4,8,128]{2,1,0:T(8,128)}, /*index=5*/bf16[128,8,128]{2,1,0:T(8,128)(2,1)}) custom-call(f32[24,64]{1,0:T(8,128)} %get-tuple-element.18.refs_0_, f32[24,64]{1,0:T(8,128)} %get-tuple-element.19.refs_1_, ...), custom_call_target="tpu_custom_call" | custom-call | tf_op jit(solution)/shard_map/pallas_call | solution.py:1038

commit v6 on v5

--- a/solution.py
+++ b/solution.py
@@ -86,10 +86,6 @@
     recv_pick_t,
     xp,
     xp_t,
-    row_src,
-    row_dst,
-    col_src,
-    col_dst,
     ex_src,
     ex_dst,
     low_in,
@@ -377,7 +373,7 @@
             line = orders[1, pl.ds(a, 1), :].astype(F32)
             column = jnp.broadcast_to(line, (LANES, LANES)).T
             for t in range(rows):
-                index = recv_index(lane + t * LANES)
+                index = (lane + t * LANES).astype(F32)
                 recv_pick[
                     pl.ds(pl.multiple_of(a * LANES, LANES), LANES), t * LANES : (t + 1) * LANES
                 ] = jnp.where(column == index, 1.0, 0.0).astype(BF16)
@@ -397,46 +393,13 @@
 
         lax.fori_loop(0, rows, body, 0)
 
-    def regroup(values):
-        m = values.shape[0] // 2
-        n = values.shape[1] // portion
-        low, high = values[:m], values[m:]
-        parts = []
-        for value in (jnp.where(first, low, swap(high)), jnp.where(first, swap(low), high)):
-            for k in range(n):
-                block = value[:, k * portion : (k + 1) * portion, :]
-                parts.append(block.reshape(m * portion, LANES))
-        return parts
-
-    def row_copy(k):
-        other = lax.rem(r + k, n_row)
-        return pltpu.make_async_remote_copy(
-            src_ref=row_src.at[other],
-            dst_ref=row_dst.at[r],
-            send_sem=as_sem.at[0],
-            recv_sem=ar_sem.at[0],
-            device_id=(other, c),
-            device_id_type=MESH,
-        )
-
-    def col_copy(k):
-        other = lax.rem(c + k, n_col)
-        return pltpu.make_async_remote_copy(
-            src_ref=col_src.at[other],
-            dst_ref=col_dst.at[c],
-            send_sem=as_sem.at[1],
-            recv_sem=ar_sem.at[1],
-            device_id=(r, other),
-            device_id_type=MESH,
-        )
-
-    def ex_copy(k):
+    def ex_copy(which, k):
         other = lax.rem(me + k, n_dev)
         return pltpu.make_async_remote_copy(
-            src_ref=ex_src.at[other],
-            dst_ref=ex_dst.at[me],
-            send_sem=as_sem.at[2],
-            recv_sem=ar_sem.at[2],
+            src_ref=ex_src.at[which, other],
+            dst_ref=ex_dst.at[which, me],
+            send_sem=as_sem.at[which],
+            recv_sem=ar_sem.at[which],
             device_id=(other // n_col, lax.rem(other, n_col)),
             device_id_type=MESH,
         )
@@ -453,18 +416,18 @@
         pltpu.make_async_copy(most, most, recv_sem).wait()
         pltpu.make_async_copy(most, most, send_sem).wait()
 
-    def recv_index(position):
-        slot = lax.rem(position, portion)
-        rest = position // portion
-        low_row = lax.rem(rest, n_row // 2)
-        rest = rest // (n_row // 2)
-        col = lax.rem(rest, n_col)
-        row = (rest // n_col) * (n_row // 2) + low_row
-        return (((row * n_col) + col) * portion + slot).astype(F32)
+    def ex_start(which):
+        peers(n_dev, functools.partial(ex_copy, which))
+        ex_dst[which, me] = ex_src[which, me]
+
+    def ex_wait(which):
+        drain(ex_dst.at[which], n_dev, as_sem.at[which], ar_sem.at[which])
+        return ex_dst[which].reshape(bins, LANES)
 
     loads[0].wait()
     loads[1].wait()
     build_send()
+    build_recv()
     for way in range(8):
 
         @pl.when(jnp.logical_not(present(way)))
@@ -492,27 +455,19 @@
     flat = dot(wcat[...], x[...], 1, 1)
     xp_t[...] = flat
     picked = dot(flat.astype(BF16), send_pick[...], 1, 1)
-    turned = jnp.concatenate(
-        [picked[:, i * LANES : (i + 1) * LANES].T for i in range(rows)], axis=0
-    ).reshape(n_row, 2, n_col // 2 * portion, LANES)
-    row_src[...] = jnp.where(first, swap(turned[:, 0]), turned[:, 1]).astype(BF16)
+    each_dev = LANES // portion
+    for i in range(rows):
+        block = picked[:, i * LANES : (i + 1) * LANES].T.astype(BF16)
+        ex_src[0, i * each_dev : (i + 1) * each_dev] = block.reshape(each_dev, portion, LANES)
 
     pl.semaphore_wait(meet_sem, n_col - 1)
-
-    peers(n_row, row_copy)
-    row_dst[r] = row_src[r]
 
     for i in range(rows):
         block = xp_t[:, i * LANES : (i + 1) * LANES].T
         xp[bins_of(i), :] = block
         put(0, i, swap(block.astype(BF16).astype(F32)))
     halo_start(0)
-    build_recv()
-    drain(row_dst, n_row, as_sem.at[0], ar_sem.at[0])
-    for k, value in enumerate(regroup(row_dst[...].astype(F32))):
-        col_src[k] = value.astype(BF16)
-    peers(n_col, col_copy)
-    col_dst[c] = col_src[c]
+    ex_start(0)
 
     def elu(value):
         return jnp.where(value > 0, value, jnp.exp(jnp.minimum(value, 0.0)) - 1.0)
@@ -524,14 +479,11 @@
     halo_take(0)
     stencil(0, first_latent)
 
-    drain(col_dst, n_col, as_sem.at[1], ar_sem.at[1])
-    low_in[...] = col_dst[...].reshape(bins // 2, LANES)
+    low_in[...] = ex_wait(0)
 
     def pick_in(i):
         here = bins_of(i, chunk)
-        value = swap(dot(recv_pick[here, : bins // 2], low_in[...])) + dot(
-            recv_pick[here, bins // 2 :], low_in[...]
-        )
+        value = dot(recv_pick[here, :], low_in[...])
         for k in range(rows // CHUNKS):
             at = i * (rows // CHUNKS) + k
             put(1, at, jnp.where(first, emb[at], value[k * LANES : (k + 1) * LANES, :]))
@@ -658,7 +610,8 @@
         total = rs2_dst[which, 0].astype(F32)
         for k in range(1, n_col):
             total += rs2_dst[which, k].astype(F32)
-        norm_src[which] = jnp.broadcast_to(jnp.sum(total * total), (8, LANES))
+        squares = jnp.broadcast_to(jnp.sum(total * total), (1, LANES))
+        norm_src[...] = jnp.where(first, norm_src[...], squares) if which else squares
         pairs = total[lats:, :]
         pairs = jnp.concatenate([pairs, swap(pairs)], axis=0).T
         by_gene[pl.ds(pl.multiple_of(core * lats, lats), LANES), :] = total[:lats, :].T
@@ -800,8 +753,8 @@
 
     disc_b[r] = disc_bsrc[...]
     peers(n_row, disc_2)
+    halo_take(4)
     rs1_start(0)
-    halo_take(4)
 
     def to_proj_grad(i, value):
         pg_low[bins_of(i), :] = value.astype(BF16)
@@ -810,13 +763,12 @@
 
     def pick_back(i):
         value = dot(recv_pick_t[bins_of(i, chunk), :], pg_low[...])
-        ex_src[pl.ds(i * (n_dev // CHUNKS), n_dev // CHUNKS)] = value.astype(BF16).reshape(
+        ex_src[1, pl.ds(i * (n_dev // CHUNKS), n_dev // CHUNKS)] = value.astype(BF16).reshape(
             n_dev // CHUNKS, portion, LANES
         )
 
     each(CHUNKS, pick_back)
-    peers(n_dev, ex_copy)
-    ex_dst[me] = ex_src[me]
+    ex_start(1)
     for i in range(rows):
         here = slice(i * LANES, (i + 1) * LANES)
         flipped = pg_low[here, :].astype(F32).T
@@ -846,9 +798,8 @@
         halo_finish(turn)
 
     lt[0:lats, :] = own[...]
-    drain(ex_dst, n_dev, as_sem.at[2], ar_sem.at[2])
+    home = ex_wait(1)
     rs2_start(0)
-    home = ex_dst[...].reshape(bins, LANES)
     flipped = jnp.concatenate(
         [home[i * LANES : (i + 1) * LANES, :].astype(F32).T[lats:, :] for i in range(rows)], axis=1
     ).astype(BF16)
@@ -886,10 +837,12 @@
     norm_a[r] = norm_src[...]
     peers(n_row, norm_1)
     drain(norm_a, n_row, ns_sem.at[0], nr_sem.at[0])
-    totals = jnp.sum(norm_a[...], axis=0)
+    totals = norm_a[0]
+    for k in range(1, n_row):
+        totals += norm_a[k]
     entries = genes * lats
-    enc_out[...] = enc_sum * lax.rsqrt(totals[1, 0:1, 0:1] / entries + 1e-06)
-    dec_out[...] = dec_sum[...] * lax.rsqrt(totals[0, 0:1, 0:1] / entries + 1e-06)
+    enc_out[...] = enc_sum * lax.rsqrt(totals[0:1, lats : lats + 1] / entries + 1e-06)
+    dec_out[...] = dec_sum[...] * lax.rsqrt(totals[0:1, 0:1] / entries + 1e-06)
     outs[0].start()
     outs[1].start()
     for out in outs:
@@ -951,13 +904,9 @@
         vmem((bins, bins), BF16),
         vmem((bins, LANES), F32),
         vmem((LANES, bins), F32),
-        vmem((n_row, n_col // 2 * portion, LANES), BF16),
-        vmem((n_row, n_col // 2 * portion, LANES), BF16),
-        vmem((n_col, n_row // 2 * portion, LANES), BF16),
-        vmem((n_col, n_row // 2 * portion, LANES), BF16),
-        vmem((n_dev, portion, LANES), BF16),
-        vmem((n_dev, portion, LANES), BF16),
-        vmem((bins // 2, LANES), BF16),
+        vmem((2, n_dev, portion, LANES), BF16),
+        vmem((2, n_dev, portion, LANES), BF16),
+        vmem((bins, LANES), BF16),
         vmem((2, tile_rows + 2 * RADIUS, LANES + 2 * SIDE, LANES), F32),
         vmem((tile_rows, LANES + 2 * SIDE, LANES), F32),
         vmem((ROUNDS,) + field, BF16),
@@ -993,8 +942,8 @@
         vmem((part, LANES), F32),
         vmem((n_row, part, LANES), F32),
         vmem((n_col, part, LANES), F32),
-        vmem((2, 8, LANES), F32),
-        vmem((n_row, 2, 8, LANES), F32),
+        vmem((1, LANES), F32),
+        vmem((n_row, 1, LANES), F32),
         vmem((span // 2, lats), F32),
         vmem((LANES, tile_rows, LANES), F32),
         vmem((per_dev, lats), F32),
@@ -1002,8 +951,8 @@
         dma((tile_rows,)),
         dma((ROUNDS, 8)),
         dma((ROUNDS, 8)),
-        dma((3,)),
-        dma((3,)),
+        dma((2,)),
+        dma((2,)),
         dma((2, 2)),
         dma((2, 2)),
         dma((2,)),

time: 83.7 us -> 80.9 us (0.967)
  Pallas kernels: 82.8 us -> 80.1 us
    pallas_call x1, Pallas kernels: 80.9 us -> 78.2 us  [per_device(): pl.pallas_call(functools.partial(kernel, n_row, n_col), out_shape=out_sha...]
where the time goes in v6:
time: 80.9 us; the launch traced here: 80.8 us
  Pallas kernels  80.1 us (99%)
    pallas_call x1, Pallas kernels, per_device(): pl.pallas_call(functools.partial(kernel, n_row, n_col), out_shape=out_sha...  78.2 us
    pallas_call x1, Pallas kernels, per_device(): pl.pallas_call(hand_on, out_shape=out_shape, in_specs=anywhere, out_specs...  1.91 us

profile of v6, /device:TPU:1, one launch (start us, length us, event | category | flops | bytes accessed | tf_op | source)
XLA Modules:
  0.0 80.8 jit_solution(3038612261643634699)
XLA Ops:
  0.6 78.2 %shard_map.109 = (f32[24,64]{1,0:T(8,128)}, f32[24,64]{1,0:T(8,128)}, f32[64,64]{1,0:T(8,128)}, f32[64,8,128]{2,1,0:T(8,128)}, f32[4,8,128]{2,1,0:T(8,128)}, /*index=5*/bf16[128,8,128]{2,1,0:T(8,128)(2,1)}) custom-call(bf16[1024,3072]{1,0:T(8,128)(2,1)} %bitcast.6, bf16[64,3072]{1,0:T(8,128)(2,1)} %bitcast.7, bf16[64,3072]{1,0:T(8,128)(2,1)} %bitcast.8, ...), custom_call_target="tpu_custom_call" | custom-call | tf_op jit(solution)/shard_map/pallas_call | solution.py:970
  78.8 1.9 %shard_map.110 = (f32[24,64]{1,0:T(8,128)}, f32[24,64]{1,0:T(8,128)}, f32[64,64]{1,0:T(8,128)}, f32[64,8,128]{2,1,0:T(8,128)}, f32[4,8,128]{2,1,0:T(8,128)}, /*index=5*/bf16[128,8,128]{2,1,0:T(8,128)(2,1)}) custom-call(f32[24,64]{1,0:T(8,128)} %get-tuple-element.18.refs_0_, f32[24,64]{1,0:T(8,128)} %get-tuple-element.19.refs_1_, ...), custom_call_target="tpu_custom_call" | custom-call | tf_op jit(solution)/shard_map/pallas_call | solution.py:987

commit v7 on v6

--- a/solution.py
+++ b/solution.py
@@ -12,6 +12,8 @@
 RECON_WEIGHT = 10.0
 LANES = 128
 SIDE = 8
+STRIDE = 37
+UNROLL = 8
 MESH = pl.DeviceIdType.MESH
 F32 = jnp.float32
 BF16 = jnp.bfloat16
@@ -394,7 +396,7 @@
         lax.fori_loop(0, rows, body, 0)
 
     def ex_copy(which, k):
-        other = lax.rem(me + k, n_dev)
+        other = lax.rem(me + k * STRIDE, n_dev)
         return pltpu.make_async_remote_copy(
             src_ref=ex_src.at[which, other],
             dst_ref=ex_dst.at[which, me],
@@ -417,7 +419,13 @@
         pltpu.make_async_copy(most, most, send_sem).wait()
 
     def ex_start(which):
-        peers(n_dev, functools.partial(ex_copy, which))
+        def several(i):
+            for k in range(UNROLL):
+                ex_copy(which, i * UNROLL + k).start()
+
+        for k in range(1, UNROLL):
+            ex_copy(which, k).start()
+        each(n_dev // UNROLL - 1, lambda i: several(i + 1))
         ex_dst[which, me] = ex_src[which, me]
 
     def ex_wait(which):

time: 80.9 us -> 81.1 us (level)
  no operation moved by 1% of the time
where the time goes in v7:
time: 81.1 us; the launch traced here: 80.9 us
  Pallas kernels  80.3 us (99%)
    pallas_call x1, Pallas kernels, per_device(): pl.pallas_call(functools.partial(kernel, n_row, n_col), out_shape=out_sha...  78.4 us
    pallas_call x1, Pallas kernels, per_device(): pl.pallas_call(hand_on, out_shape=out_shape, in_specs=anywhere, out_specs...  1.91 us

profile of v7, /device:TPU:1, one launch (start us, length us, event | category | flops | bytes accessed | tf_op | source)
XLA Modules:
  0.0 80.9 jit_solution(1056348460352601841)
XLA Ops:
  0.6 78.4 %shard_map.109 = (f32[24,64]{1,0:T(8,128)}, f32[24,64]{1,0:T(8,128)}, f32[64,64]{1,0:T(8,128)}, f32[64,8,128]{2,1,0:T(8,128)}, f32[4,8,128]{2,1,0:T(8,128)}, /*index=5*/bf16[128,8,128]{2,1,0:T(8,128)(2,1)}) custom-call(bf16[1024,3072]{1,0:T(8,128)(2,1)} %bitcast.6, bf16[64,3072]{1,0:T(8,128)(2,1)} %bitcast.7, bf16[64,3072]{1,0:T(8,128)(2,1)} %bitcast.8, ...), custom_call_target="tpu_custom_call" | custom-call | tf_op jit(solution)/shard_map/pallas_call | solution.py:978
  79.0 1.9 %shard_map.110 = (f32[24,64]{1,0:T(8,128)}, f32[24,64]{1,0:T(8,128)}, f32[64,64]{1,0:T(8,128)}, f32[64,8,128]{2,1,0:T(8,128)}, f32[4,8,128]{2,1,0:T(8,128)}, /*index=5*/bf16[128,8,128]{2,1,0:T(8,128)(2,1)}) custom-call(f32[24,64]{1,0:T(8,128)} %get-tuple-element.18.refs_0_, f32[24,64]{1,0:T(8,128)} %get-tuple-element.19.refs_1_, ...), custom_call_target="tpu_custom_call" | custom-call | tf_op jit(solution)/shard_map/pallas_call | solution.py:995

commit v8 on v7

--- a/solution.py
+++ b/solution.py
@@ -418,6 +418,11 @@
         pltpu.make_async_copy(most, most, recv_sem).wait()
         pltpu.make_async_copy(most, most, send_sem).wait()
 
+    def ex_pack(values):
+        values = values.reshape(-1, portion, LANES)
+        half = portion // 2
+        return jnp.where(first, swap(values[:, :half, :]), values[:, half:, :]).astype(BF16)
+
     def ex_start(which):
         def several(i):
             for k in range(UNROLL):
@@ -430,7 +435,9 @@
 
     def ex_wait(which):
         drain(ex_dst.at[which], n_dev, as_sem.at[which], ar_sem.at[which])
-        return ex_dst[which].reshape(bins, LANES)
+        values = ex_dst[which].astype(F32)
+        values = jnp.concatenate([swap(values), values], axis=1)
+        return values.reshape(bins, LANES).astype(BF16)
 
     loads[0].wait()
     loads[1].wait()
@@ -465,8 +472,8 @@
     picked = dot(flat.astype(BF16), send_pick[...], 1, 1)
     each_dev = LANES // portion
     for i in range(rows):
-        block = picked[:, i * LANES : (i + 1) * LANES].T.astype(BF16)
-        ex_src[0, i * each_dev : (i + 1) * each_dev] = block.reshape(each_dev, portion, LANES)
+        block = picked[:, i * LANES : (i + 1) * LANES].T
+        ex_src[0, i * each_dev : (i + 1) * each_dev] = ex_pack(block)
 
     pl.semaphore_wait(meet_sem, n_col - 1)
 
@@ -771,9 +778,7 @@
 
     def pick_back(i):
         value = dot(recv_pick_t[bins_of(i, chunk), :], pg_low[...])
-        ex_src[1, pl.ds(i * (n_dev // CHUNKS), n_dev // CHUNKS)] = value.astype(BF16).reshape(
-            n_dev // CHUNKS, portion, LANES
-        )
+        ex_src[1, pl.ds(i * (n_dev // CHUNKS), n_dev // CHUNKS)] = ex_pack(value)
 
     each(CHUNKS, pick_back)
     ex_start(1)
@@ -912,8 +917,8 @@
         vmem((bins, bins), BF16),
         vmem((bins, LANES), F32),
         vmem((LANES, bins), F32),
-        vmem((2, n_dev, portion, LANES), BF16),
-        vmem((2, n_dev, portion, LANES), BF16),
+        vmem((2, n_dev, portion // 2, LANES), BF16),
+        vmem((2, n_dev, portion // 2, LANES), BF16),
         vmem((bins, LANES), BF16),
         vmem((2, tile_rows + 2 * RADIUS, LANES + 2 * SIDE, LANES), F32),
         vmem((tile_rows, LANES + 2 * SIDE, LANES), F32),

time: 81.1 us -> 79.8 us (0.984)
  Pallas kernels: 80.3 us -> 79 us
    pallas_call x1, Pallas kernels: 78.4 us -> 77 us  [per_device(): pl.pallas_call(functools.partial(kernel, n_row, n_col), out_shape=out_sha...]
where the time goes in v8:
time: 79.8 us; the launch traced here: 79.6 us
  Pallas kernels  79 us (99%)
    pallas_call x1, Pallas kernels, per_device(): pl.pallas_call(functools.partial(kernel, n_row, n_col), out_shape=out_sha...  77 us
    pallas_call x1, Pallas kernels, per_device(): pl.pallas_call(hand_on, out_shape=out_shape, in_specs=anywhere, out_specs...  1.91 us

profile of v8, /device:TPU:1, one launch (start us, length us, event | category | flops | bytes accessed | tf_op | source)
XLA Modules:
  0.0 79.6 jit_solution(17068349205347902384)
XLA Ops:
  0.6 77.0 %shard_map.109 = (f32[24,64]{1,0:T(8,128)}, f32[24,64]{1,0:T(8,128)}, f32[64,64]{1,0:T(8,128)}, f32[64,8,128]{2,1,0:T(8,128)}, f32[4,8,128]{2,1,0:T(8,128)}, /*index=5*/bf16[128,8,128]{2,1,0:T(8,128)(2,1)}) custom-call(bf16[1024,3072]{1,0:T(8,128)(2,1)} %bitcast.6, bf16[64,3072]{1,0:T(8,128)(2,1)} %bitcast.7, bf16[64,3072]{1,0:T(8,128)(2,1)} %bitcast.8, ...), custom_call_target="tpu_custom_call" | custom-call | tf_op jit(solution)/shard_map/pallas_call | solution.py:983
  77.7 1.9 %shard_map.110 = (f32[24,64]{1,0:T(8,128)}, f32[24,64]{1,0:T(8,128)}, f32[64,64]{1,0:T(8,128)}, f32[64,8,128]{2,1,0:T(8,128)}, f32[4,8,128]{2,1,0:T(8,128)}, /*index=5*/bf16[128,8,128]{2,1,0:T(8,128)(2,1)}) custom-call(f32[24,64]{1,0:T(8,128)} %get-tuple-element.18.refs_0_, f32[24,64]{1,0:T(8,128)} %get-tuple-element.19.refs_1_, ...), custom_call_target="tpu_custom_call" | custom-call | tf_op jit(solution)/shard_map/pallas_call | solution.py:1000

commit v9 on v8

--- a/solution.py
+++ b/solution.py
@@ -696,35 +696,6 @@
         contrast(i)
     halo_start(3)
 
-    def disc_step(i, total):
-        here = bins_of(i, chunk)
-        return total + dot(grads_2[here, :], summ_2[here, :], 0, 0)
-
-    disc_total = lax.fori_loop(
-        0, CHUNKS, disc_step, jnp.zeros((2 * LANES, 2 * LANES), F32)
-    )
-    quarter = (disc_total[:LANES, :LANES] + disc_total[LANES:, :LANES]) + (
-        disc_total[:LANES, LANES:] + disc_total[LANES:, LANES:]
-    )
-    disc_src[...] = quarter[:lats, :] + swap(quarter[lats:, :])
-
-    def part_of(index):
-        return pl.ds(pl.multiple_of(index * part, 8), part)
-
-    def disc_1(k):
-        other = lax.rem(c + k, n_col)
-        return pltpu.make_async_remote_copy(
-            src_ref=disc_src.at[part_of(other)],
-            dst_ref=disc_a.at[c],
-            send_sem=ds_sem.at[0],
-            recv_sem=dr_sem.at[0],
-            device_id=(r, other),
-            device_id_type=MESH,
-        )
-
-    disc_a[c] = disc_src[part_of(c), :]
-    peers(n_col, disc_1)
-
     for i in range(rows):
         flipped = mix[i * LANES : (i + 1) * LANES, :].T
         for k in range(4):
@@ -752,6 +723,58 @@
     stencil(3, to_latent_grad)
     halo_start(4)
 
+    def disc_step(i, total):
+        here = bins_of(i, chunk)
+        return total + dot(grads_2[here, :], summ_2[here, :], 0, 0)
+
+    disc_total = lax.fori_loop(
+        0, CHUNKS, disc_step, jnp.zeros((2 * LANES, 2 * LANES), F32)
+    )
+    quarter = (disc_total[:LANES, :LANES] + disc_total[LANES:, :LANES]) + (
+        disc_total[:LANES, LANES:] + disc_total[LANES:, LANES:]
+    )
+    disc_src[...] = quarter[:lats, :] + swap(quarter[lats:, :])
+
+    def part_of(index):
+        return pl.ds(pl.multiple_of(index * part, 8), part)
+
+    def disc_1(k):
+        other = lax.rem(c + k, n_col)
+        return pltpu.make_async_remote_copy(
+            src_ref=disc_src.at[part_of(other)],
+            dst_ref=disc_a.at[c],
+            send_sem=ds_sem.at[0],
+            recv_sem=dr_sem.at[0],
+            device_id=(r, other),
+            device_id_type=MESH,
+        )
+
+    disc_a[c] = disc_src[part_of(c), :]
+    peers(n_col, disc_1)
+
+    halo_take(4)
+    rs1_start(0)
+
+    def to_proj_grad(i, value):
+        pg_low[bins_of(i), :] = value.astype(BF16)
+
+    stencil(4, to_proj_grad)
+
+    def pick_back(i):
+        value = dot(recv_pick_t[bins_of(i, chunk), :], pg_low[...])
+        ex_src[1, pl.ds(i * (n_dev // CHUNKS), n_dev // CHUNKS)] = ex_pack(value)
+
+    each(CHUNKS, pick_back)
+    ex_start(1)
+    for i in range(rows):
+        here = slice(i * LANES, (i + 1) * LANES)
+        flipped = pg_low[here, :].astype(F32).T
+        stage[:, i, :] = flipped
+        own[:, here] = flipped[:lats, :].astype(BF16)
+    pg_out[...] = stage[...].astype(BF16)
+    outs[5].start()
+
+    rs1_finish(0)
     drain(disc_a, n_col, ds_sem.at[0], dr_sem.at[0])
     disc_bsrc[...] = jnp.sum(disc_a[...], axis=0)
 
@@ -768,29 +791,24 @@
 
     disc_b[r] = disc_bsrc[...]
     peers(n_row, disc_2)
-    halo_take(4)
-    rs1_start(0)
-
-    def to_proj_grad(i, value):
-        pg_low[bins_of(i), :] = value.astype(BF16)
-
-    stencil(4, to_proj_grad)
-
-    def pick_back(i):
-        value = dot(recv_pick_t[bins_of(i, chunk), :], pg_low[...])
-        ex_src[1, pl.ds(i * (n_dev // CHUNKS), n_dev // CHUNKS)] = ex_pack(value)
-
-    each(CHUNKS, pick_back)
-    ex_start(1)
-    for i in range(rows):
-        here = slice(i * LANES, (i + 1) * LANES)
-        flipped = pg_low[here, :].astype(F32).T
-        stage[:, i, :] = flipped
-        own[:, here] = flipped[:lats, :].astype(BF16)
-    pg_out[...] = stage[...].astype(BF16)
-    outs[5].start()
-
-    rs1_finish(0)
+    for turn in range(ROUNDS):
+        halo_finish(turn)
+
+    lt[0:lats, :] = own[...]
+    home = ex_wait(1)
+    rs2_start(0)
+    flipped = jnp.concatenate(
+        [home[i * LANES : (i + 1) * LANES, :].astype(F32).T[lats:, :] for i in range(rows)], axis=1
+    ).astype(BF16)
+    lt[lats:, :] = dot(flipped, send_pick[...]).astype(BF16)
+
+    def encoder_part(where):
+        value = dot(lt[...], x[:, where])
+        return value[:lats, :] + value[lats:, :]
+
+    rs0_run(1, encoder_part)
+    rs1_start(1)
+
     drain(disc_b, n_row, ds_sem.at[1], dr_sem.at[1])
     disc_full[c] = jnp.sum(disc_b[...], axis=0)
 
@@ -807,33 +825,15 @@
 
     peers(n_col, disc_3)
 
-    for turn in range(ROUNDS):
-        halo_finish(turn)
-
-    lt[0:lats, :] = own[...]
-    home = ex_wait(1)
-    rs2_start(0)
-    flipped = jnp.concatenate(
-        [home[i * LANES : (i + 1) * LANES, :].astype(F32).T[lats:, :] for i in range(rows)], axis=1
-    ).astype(BF16)
-    lt[lats:, :] = dot(flipped, send_pick[...]).astype(BF16)
-
-    def encoder_part(where):
-        value = dot(lt[...], x[:, where])
-        return value[:lats, :] + value[lats:, :]
-
-    rs0_run(1, encoder_part)
-    rs1_start(1)
-
+    dec_sum[...] = rs2_finish(0)
+    rs1_finish(1)
+    rs2_start(1)
     drain(disc_full, n_col, ds_sem.at[2], dr_sem.at[2])
     disc_grad = disc_full[...].reshape(lats, LANES)[:, :lats]
     disc_mean = jnp.sum(disc_grad * disc_grad) / (lats * lats)
     disc_out[...] = disc_grad * lax.rsqrt(disc_mean + 1e-06)
     outs[2].start()
 
-    dec_sum[...] = rs2_finish(0)
-    rs1_finish(1)
-    rs2_start(1)
     enc_sum = rs2_finish(1)
 
     def norm_1(k):

time: 79.8 us -> 79.2 us (level)
  no operation moved by 1% of the time
where the time goes in v9:
time: 79.2 us; the launch traced here: 79 us
  Pallas kernels  78.4 us (99%)
    pallas_call x1, Pallas kernels, per_device(): pl.pallas_call(functools.partial(kernel, n_row, n_col), out_shape=out_sha...  76.5 us
    pallas_call x1, Pallas kernels, per_device(): pl.pallas_call(hand_on, out_shape=out_shape, in_specs=anywhere, out_specs...  1.91 us

profile of v9, /device:TPU:1, one launch (start us, length us, event | category | flops | bytes accessed | tf_op | source)
XLA Modules:
  0.0 79.0 jit_solution(12371465931858325099)
XLA Ops:
  0.6 76.5 %shard_map.109 = (f32[24,64]{1,0:T(8,128)}, f32[24,64]{1,0:T(8,128)}, f32[64,64]{1,0:T(8,128)}, f32[64,8,128]{2,1,0:T(8,128)}, f32[4,8,128]{2,1,0:T(8,128)}, /*index=5*/bf16[128,8,128]{2,1,0:T(8,128)(2,1)}) custom-call(bf16[1024,3072]{1,0:T(8,128)(2,1)} %bitcast.6, bf16[64,3072]{1,0:T(8,128)(2,1)} %bitcast.7, bf16[64,3072]{1,0:T(8,128)(2,1)} %bitcast.8, ...), custom_call_target="tpu_custom_call" | custom-call | tf_op jit(solution)/shard_map/pallas_call | solution.py:983
  77.1 1.9 %shard_map.110 = (f32[24,64]{1,0:T(8,128)}, f32[24,64]{1,0:T(8,128)}, f32[64,64]{1,0:T(8,128)}, f32[64,8,128]{2,1,0:T(8,128)}, f32[4,8,128]{2,1,0:T(8,128)}, /*index=5*/bf16[128,8,128]{2,1,0:T(8,128)(2,1)}) custom-call(f32[24,64]{1,0:T(8,128)} %get-tuple-element.18.refs_0_, f32[24,64]{1,0:T(8,128)} %get-tuple-element.19.refs_1_, ...), custom_call_target="tpu_custom_call" | custom-call | tf_op jit(solution)/shard_map/pallas_call | solution.py:1000
